TPU v7x, 32 devices: a whole 2x2x4 slice. The times are simulated.
32 devices in a mesh: dp: 4 (over z), wide: 4 (over x, core), narrow: 2 (over y).
Axes of the slice: x: 2, y: 2, z: 4, core: 2. Of those that a mesh axis runs over, the one named last changes fastest.
Arguments:
- tokens: bfloat16 [16384, 768], P(('dp', 'wide')), may hold values from -6 to 6
- memory: bfloat16 [32, 2048, 768], P(('dp', 'wide')), may hold values from -6 to 6
- cotangent: bfloat16 [16384, 768], P(('dp', 'wide')), may hold values from -6 to 6
- norm1_gain: bfloat16 [768], P('wide'), may hold values from 0.5 to 1.5
- norm2_gain: bfloat16 [768], P('wide'), may hold values from 0.5 to 1.5
- norm3_gain: bfloat16 [768], P('wide'), may hold values from 0.5 to 1.5
- q_weight: bfloat16 [768, 768], P('wide', 'narrow'), may hold values from -0.3125 to 0.3125
- k_weight: bfloat16 [768, 768], P('wide', 'narrow'), may hold values from -0.3125 to 0.3125
- v_weight: bfloat16 [768, 768], P('wide', 'narrow'), may hold values from -0.21875 to 0.21875
- o_weight: bfloat16 [768, 768], P('wide', 'narrow'), may hold values from -0.4375 to 0.4375
- cross_q: bfloat16 [768, 768], P('wide', 'narrow'), may hold values from -0.3125 to 0.3125
- cross_k: bfloat16 [768, 768], P('wide', 'narrow'), may hold values from -0.3125 to 0.3125
- cross_v: bfloat16 [768, 768], P('wide', 'narrow'), may hold values from -0.21875 to 0.21875
- cross_o: bfloat16 [768, 768], P('wide', 'narrow'), may hold values from -1.25 to 1.25
- gate_weight: bfloat16 [768, 2048], P('wide', 'narrow'), may hold values from -0.21875 to 0.21875
- up_weight: bfloat16 [768, 2048], P('wide', 'narrow'), may hold values from -0.21875 to 0.21875
- down_weight: bfloat16 [768, 2048], P('wide', 'narrow'), may hold values from -0.1875 to 0.1875
- segment_ids: int32 [16, 1024], P(('dp', 'wide')), may hold values from 0 to 7, never falling along the last dimension, each value on 1 to 256 neighbouring positions
- block_ids: int32 [16, 1024], P(('dp', 'wide')), may hold values from 0 to 63, never falling along the last dimension, each value on 1 to 32 neighbouring positions
- image_table: int32 [16, 8], P(('dp', 'wide')), may hold values from 0 to 1
Outputs:
- output: bfloat16 [16384, 768], P(('dp', 'wide'))
- tokens_grad: bfloat16 [16384, 768], P(('dp', 'wide'))
- memory_grad: bfloat16 [32, 2048, 768], P(('dp', 'wide'), None, 'narrow')
- norm1_gain_grad: float32 [768], P('wide')
- norm2_gain_grad: float32 [768], P('wide')
- norm3_gain_grad: float32 [768], P('wide')
- q_weight_grad: float32 [768, 768], P('wide', 'narrow')
- k_weight_grad: float32 [768, 768], P('wide', 'narrow')
- v_weight_grad: float32 [768, 768], P('wide', 'narrow')
- o_weight_grad: float32 [768, 768], P('wide', 'narrow')
- cross_q_grad: float32 [768, 768], P('wide', 'narrow')
- cross_k_grad: float32 [768, 768], P('wide', 'narrow')
- cross_v_grad: float32 [768, 768], P('wide', 'narrow')
- cross_o_grad: float32 [768, 768], P('wide', 'narrow')
- gate_weight_grad: float32 [768, 2048], P('wide', 'narrow')
- up_weight_grad: float32 [768, 2048], P('wide', 'narrow')
- down_weight_grad: float32 [768, 2048], P('wide', 'narrow')
Inputs may be any that keep to these rules, and one draw needn't show every extreme that they name: `segment_ids`: in each decoder row the ids never fall and every id occurs, each on 1 to 256 positions, some id on exactly that many. `block_ids`: in each decoder row the ids never fall and every id occurs, each on 1 to 32 positions, some id on exactly that many. `image_table`: entry r, s names one of the 2 images stored with decoder row r, the images r * 2 to r * 2 + 1.
All inputs are finite; a program needn't handle non-finite values.
Results may differ from a plain program's by a relative error of at most 0.038.
Values may be sent and summed in bfloat16 or wider, within the bound.
No kernel may reach another device: no remote copies, remote signals or barrier semaphores. Data moves between devices by JAX's collectives and lax.ppermute only.
A program may use at most 384 MiB of HBM per device.

v0:
```python
import functools
import math

import jax
import jax.numpy as jnp
from jax import lax
from jax.experimental import pallas as pl
from jax.experimental.pallas import tpu as pltpu
from jax.sharding import PartitionSpec as P

F32 = jnp.float32
BF16 = jnp.bfloat16
EPSILON = 1e-06
ROOT_TWO_OVER_PI = 0.7978845608028654
CUBIC = 0.044715
HEAD_DIM = 64
PAIR = 2 * HEAD_DIM
SCALE = HEAD_DIM ** (-0.5)
EXP2_SCALE = SCALE * math.log2(math.e)
HIDE = 1e30
TILE = 256
ROWS = 512
WEIGH = 4.0

NN = (((1,), (0,)), ((), ()))
NT = (((1,), (1,)), ((), ()))
TN = (((0,), (0,)), ((), ()))


def dot(left, right, dims):
    return lax.dot_general(left, right, dims, preferred_element_type=F32)


def params(mebibytes=24):
    return pltpu.CompilerParams(vmem_limit_bytes=mebibytes * 1024 * 1024)


def cost(flops, nbytes):
    return pl.CostEstimate(
        flops=int(flops * WEIGH), bytes_accessed=int(nbytes * WEIGH), transcendentals=0
    )


def pin(*arrays):
    return [pltpu.with_memory_space_constraint(array, pltpu.HBM) for array in arrays]


def shape_of(shape, dtype):
    return jax.ShapeDtypeStruct(shape, dtype)


def whole(shape):
    zeros = (0,) * len(shape)
    return pl.BlockSpec(shape, lambda *_: zeros)


def rows(width, height=None):
    height = ROWS if height is None else height
    return pl.BlockSpec((height, width), lambda t, *_: (t, 0))


def inverse_rms(values):
    return lax.rsqrt(jnp.mean(values * values, axis=1, keepdims=True) + EPSILON)


def norm_back(values, gain, upstream):
    factor = inverse_rms(values)
    scaled = upstream * gain
    mean = jnp.mean(values * scaled, axis=1, keepdims=True)
    grad = factor * scaled - values * (factor * factor * factor * mean)
    return grad, jnp.sum(upstream * values * factor, axis=0, keepdims=True)


def in_half(shape, half):
    return (lax.broadcasted_iota(jnp.int32, shape, 1) // HEAD_DIM) == half


def only_half(values, half):
    return jnp.where(in_half(values.shape, half), values, jnp.zeros_like(values))


def order_kernel(seg, blk, table, x, xp, row_ids, col_ids, pos_out, scalars, pos):
    step = pl.program_id(0)
    count = seg.shape[1]

    @pl.when(step == 0)
    def _():
        segments = seg[...]
        image = jnp.zeros_like(segments)
        for s in range(table.shape[1]):
            image = jnp.where(segments == s, table[0, s], image)
        first = (image == 0).astype(F32)
        before = lax.broadcasted_iota(jnp.int32, (count, count), 0) < lax.broadcasted_iota(
            jnp.int32, (count, count), 1
        )
        rank = dot(
            jnp.broadcast_to(first, (8, count)).astype(BF16),
            before.astype(F32).astype(BF16),
            NN,
        )[0:1]
        total = jnp.sum(first)
        index = lax.broadcasted_iota(jnp.int32, (1, count), 1).astype(F32)
        place = jnp.where(image == 0, rank, total + index - rank)
        pos[...] = place.astype(jnp.int32)
        pos_out[...] = jnp.broadcast_to(pos[...], (8, count))
        n0 = total.astype(jnp.int32)
        tiles = count // TILE
        visits0 = jnp.maximum(1, (n0 + TILE - 1) // TILE)
        start1 = jnp.minimum(tiles - 1, n0 // TILE)
        visits = visits0 + tiles - start1
        for v in range(tiles + 1):
            real = jnp.minimum(v, visits - 1)
            in_first = real < visits0
            scalars[v] = jnp.where(in_first, real, real - visits0 + start1)
            scalars[8 + v] = jnp.where(in_first, 0, 1)
        scalars[16] = visits
        scalars[17] = n0
        scalars[18] = visits0
        scalars[19] = start1
        scalars[20] = tiles - start1

    onehot = (
        lax.broadcasted_iota(jnp.int32, (TILE, count), 0) + step * TILE == pos[...]
    ).astype(F32).astype(BF16)
    xp[...] = dot(onehot, x[...], NN).astype(BF16)
    ids = jnp.concatenate(
        [
            seg[...].astype(F32),
            blk[...].astype(F32),
            jnp.zeros((126, count), F32),
        ],
        axis=0,
    ).astype(BF16)
    row_ids[...] = dot(ids[0:8], onehot, NT)
    col_ids[...] = dot(onehot, ids, NT)


def order_rows(seg, blk, table, x):
    count, width = x.shape
    return pl.pallas_call(
        order_kernel,
        grid=(count // TILE,),
        in_specs=[
            whole((1, count)),
            whole((1, count)),
            pl.BlockSpec(memory_space=pltpu.SMEM),
            whole((count, width)),
        ],
        out_specs=[
            rows(width, TILE),
            pl.BlockSpec((8, TILE), lambda t: (0, t)),
            rows(128, TILE),
            whole((8, count)),
            pl.BlockSpec(memory_space=pltpu.SMEM),
        ],
        out_shape=[
            pltpu.HBM((count, width), BF16),
            shape_of((8, count), F32),
            shape_of((count, 128), F32),
            shape_of((8, count), jnp.int32),
            shape_of((32,), jnp.int32),
        ],
        scratch_shapes=[pltpu.VMEM((1, count), jnp.int32)],
        compiler_params=params(),
        cost_estimate=cost(2 * count * count * width, 8 * count * width),
    )(seg, blk, table, *pin(x))


def order_more_kernel(pos, values, out):
    size, count = out.shape[0], values.shape[0]
    index = lax.broadcasted_iota(jnp.int32, (size, count), 0) + pl.program_id(0) * size
    onehot = (index == pos[0:1, :]).astype(F32).astype(BF16)
    out[...] = dot(onehot, values[...], NN).astype(BF16)


def order_more(pos, values):
    count, width = values.shape
    return pl.pallas_call(
        order_more_kernel,
        grid=(count // TILE,),
        in_specs=[whole((8, count)), whole((count, width))],
        out_specs=rows(width, TILE),
        out_shape=pltpu.HBM((count, width), BF16),
        compiler_params=params(),
        cost_estimate=cost(2 * count * count * width, 4 * count * width),
    )(pos, *pin(values))


def restore_kernel(pos, values, out):
    count = values.shape[0]
    onehot = (
        lax.broadcasted_iota(jnp.int32, (count, TILE), 0) == pos[0:1, :]
    ).astype(F32).astype(BF16)
    out[...] = dot(onehot, values[...], TN).astype(BF16)


def restore_rows(pos, values):
    count, width = values.shape
    return pl.pallas_call(
        restore_kernel,
        grid=(count // TILE,),
        in_specs=[pl.BlockSpec((8, TILE), lambda t: (0, t)), whole((count, width))],
        out_specs=rows(width, TILE),
        out_shape=shape_of((count, width), BF16),
        compiler_params=params(),
        cost_estimate=cost(2 * count * count * width, 4 * count * width),
    )(pos, *pin(values))


def fetch(pieces, places, columns, dest, sems, base=0):
    height = dest.shape[0] // 4
    copies = []
    for i, piece in enumerate(pieces):
        start = pl.multiple_of(places[i] * height, 16)
        copies.append(
            pltpu.make_async_copy(
                piece.at[pl.ds(0, height), columns],
                dest.at[pl.ds(start, height), :],
                sems.at[base + i],
            )
        )
    return copies


def fetch_half(gathered, half, columns, dest, sem):
    return pltpu.make_async_copy(gathered.at[half, :, columns], dest, sem)


def start_all(copies):
    for copy in copies:
        copy.start()


def wait_all(copies):
    for copy in copies:
        copy.wait()


ANY = pl.BlockSpec(memory_space=pl.ANY)
SCALARS = pl.BlockSpec(memory_space=pltpu.SMEM)


def project_kernel(places, x, gain, w0, w1, w2, w3, normed, out, weight, sems):
    @pl.when(pl.program_id(0) == 0)
    def _():
        copies = fetch((w0, w1, w2, w3), places, slice(0, weight.shape[1]), weight, sems)
        start_all(copies)
        wait_all(copies)

    values = x[...].astype(F32)
    n1 = (values * inverse_rms(values) * gain[...]).astype(BF16)
    normed[...] = n1
    out[...] = dot(n1, weight[...], NN).astype(BF16)


def norm_project(places, x, gain, pieces):
    count, width = x.shape
    outs = pieces[0].shape[1]
    return pl.pallas_call(
        project_kernel,
        grid=(count // ROWS,),
        in_specs=[SCALARS, rows(width), whole((1, width))] + [ANY] * 4,
        out_specs=[rows(width), rows(outs)],
        out_shape=[pltpu.HBM((count, width), BF16), shape_of((count, outs), BF16)],
        scratch_shapes=[pltpu.VMEM((width, outs), BF16), pltpu.SemaphoreType.DMA((4,))],
        compiler_params=params(),
        cost_estimate=cost(2 * count * width * outs, 4 * count * width + 2 * count * outs),
    )(places, *pin(x), gain, *pieces)


MEMORY_TILE = 1024
BACK_TILE = 512


def memory_kernel(places, columns, memory, w0, w1, w2, w3, out, weight, sems):
    @pl.when(pl.program_id(0) == 0)
    def _():
        copies = fetch((w0, w1, w2, w3), places, columns, weight, sems)
        start_all(copies)
        wait_all(copies)

    out[...] = dot(memory[...], weight[...], NN).astype(BF16)


def project_memory(places, memory, pieces, columns):
    count, width = memory.shape
    outs = columns.stop - columns.start

    def kernel(places, *refs):
        memory_kernel(places, columns, *refs)

    return pl.pallas_call(
        kernel,
        grid=(count // MEMORY_TILE,),
        in_specs=[SCALARS, rows(width, MEMORY_TILE)] + [ANY] * 4,
        out_specs=rows(outs, MEMORY_TILE),
        out_shape=pltpu.HBM((count, outs), BF16),
        scratch_shapes=[pltpu.VMEM((width, outs), BF16), pltpu.SemaphoreType.DMA((4,))],
        compiler_params=params(),
        cost_estimate=cost(2 * count * width * outs, 4 * count * width),
    )(places, *pin(memory), *pieces)


SELF_TILE = 256
SELF_WINDOW = 640
BACK_WINDOW = 640


def store_logs(ref, columns, logs, extra=None):
    spread = jnp.where(in_half((logs[0].shape[0], PAIR), 0), logs[0], logs[1]).T
    for half in range(2):
        line = spread[half * HEAD_DIM : half * HEAD_DIM + 1, :]
        if extra is not None:
            line = jnp.where(extra, line, ref[half : half + 1, columns])
        ref[half : half + 1, columns] = line


def self_forward_kernel(q, k, v, row_ids, col_ids, out, logs):
    count = q.shape[0]
    for tile in range(count // SELF_TILE):
        base = tile * SELF_TILE
        start = min(max(base - 256, 0), count - SELF_WINDOW)
        spot = slice(base, base + SELF_TILE)
        window = slice(start, start + SELF_WINDOW)
        seen = (col_ids[spot, 0:1] == row_ids[0:1, window]) & (
            row_ids[1:2, window] <= col_ids[spot, 1:2]
        )
        bias = jnp.where(seen, 0.0, -HIDE)
        keys = k[window, :]
        values = v[window, :]
        queries = q[spot, :]
        parts, totals = [], []
        for half in range(2):
            scores = dot(only_half(queries, half), keys, NT) * EXP2_SCALE + bias
            highest = jnp.max(scores, axis=1, keepdims=True)
            weights = jnp.exp2(scores - highest)
            total = jnp.sum(weights, axis=1, keepdims=True)
            parts.append(dot(weights.astype(BF16), values, NN) / total)
            totals.append(highest + jnp.log2(total))
        out[spot, :] = jnp.where(in_half(parts[0].shape, 0), parts[0], parts[1]).astype(BF16)
        store_logs(logs, spot, totals)


def self_forward(pair, qkv, row_ids, col_ids):
    count = qkv.shape[0]
    pairs = qkv.shape[1] // (3 * PAIR)

    def part(which):
        return pl.BlockSpec((count, PAIR), lambda p: (0, which * pairs + pair))

    return pl.pallas_call(
        self_forward_kernel,
        grid=(1,),
        in_specs=[part(0), part(1), part(2), whole((8, count)), whole((count, 128))],
        out_specs=[whole((count, PAIR)), whole((8, count))],
        out_shape=[pltpu.HBM((count, PAIR), BF16), pltpu.HBM((8, count), F32)],
        compiler_params=params(),
        cost_estimate=cost(16 * count * SELF_WINDOW * PAIR, 8 * count * PAIR),
    )(qkv, qkv, qkv, row_ids, col_ids)


def self_backward_kernel(q, k, v, grad, logs, deltas, row_ids, col_ids, dq, dk, dv, key_sum, value_sum):
    count = q.shape[0]
    key_sum[...] = jnp.zeros_like(key_sum)
    value_sum[...] = jnp.zeros_like(value_sum)
    for tile in range(count // TILE):
        base = tile * TILE
        start = min(max(base - 256, 0), count - BACK_WINDOW)
        spot = slice(base, base + TILE)
        window = slice(start, start + BACK_WINDOW)
        seen = (col_ids[window, 0:1] == row_ids[0:1, spot]) & (
            col_ids[window, 1:2] <= row_ids[1:2, spot]
        )
        bias = jnp.where(seen, 0.0, -HIDE)
        keys = k[window, :]
        values = v[window, :]
        queries = q[spot, :]
        grads = grad[spot, :]
        parts = []
        for half in range(2):
            one_query = only_half(queries, half)
            one_grad = only_half(grads, half)
            scores = dot(keys, one_query, NT) * EXP2_SCALE + bias
            weights = jnp.exp2(scores - logs[half : half + 1, spot])
            slopes = dot(values, one_grad, NT)
            pushed = (weights * (slopes - deltas[half : half + 1, spot])).astype(BF16)
            value_sum[window, :] += dot(weights.astype(BF16), one_grad, NN)
            key_sum[window, :] += dot(pushed, one_query, NN)
            parts.append(dot(pushed, keys, TN))
        dq[spot, :] = (
            jnp.where(in_half(parts[0].shape, 0), parts[0], parts[1]) * SCALE
        ).astype(BF16)
    dk[...] = (key_sum[...] * SCALE).astype(BF16)
    dv[...] = value_sum[...].astype(BF16)


def self_backward(pair, qkv, grad, logs, deltas, row_ids, col_ids):
    count = qkv.shape[0]
    pairs = qkv.shape[1] // (3 * PAIR)

    def part(which):
        return pl.BlockSpec((count, PAIR), lambda p: (0, which * pairs + pair))

    return pl.pallas_call(
        self_backward_kernel,
        grid=(1,),
        in_specs=[
            part(0),
            part(1),
            part(2),
            part(0),
            whole((8, count)),
            pl.BlockSpec((8, count), lambda p: (pair, 0)),
            whole((8, count)),
            whole((count, 128)),
        ],
        out_specs=[whole((count, PAIR))] * 3,
        out_shape=[pltpu.HBM((count, PAIR), BF16)] * 3,
        scratch_shapes=[pltpu.VMEM((count, PAIR), F32)] * 2,
        compiler_params=params(),
        cost_estimate=cost(40 * count * BACK_WINDOW * PAIR, 16 * count * PAIR),
    )(qkv, qkv, qkv, grad, logs, deltas, row_ids, col_ids)


KEYS = 1024


def visits_of(image, scalars):
    first = jnp.where(image == 0, 0, scalars[19])
    return first, jnp.where(image == 0, scalars[18], scalars[20])


def cross_forward_kernel(scalars, q, k, v, out, logs):
    image = pl.program_id(0)
    first, count = visits_of(image, scalars)

    def visit(i, carry):
        base = pl.multiple_of((first + i) * TILE, TILE)
        spot = pl.ds(base, TILE)
        queries = q[spot, :]
        parts, totals = [], []
        tops, sums = [None, None], [None, None]
        for start in range(0, k.shape[0], KEYS):
            keys = k[start : start + KEYS, :]
            values = v[start : start + KEYS, :]
            both = [dot(only_half(queries, half), keys, NT) for half in range(2)]
            for half, scores in enumerate(both):
                highest = jnp.max(scores, axis=1, keepdims=True) * EXP2_SCALE
                if start:
                    highest = jnp.maximum(highest, tops[half])
                weights = jnp.exp2(scores * EXP2_SCALE - highest).astype(BF16)
                mixed = dot(
                    weights,
                    jnp.where(in_half(values.shape, half), values, jnp.ones_like(values)),
                    NN,
                )
                if start:
                    mixed = mixed + sums[half] * jnp.exp2(tops[half] - highest)
                tops[half], sums[half] = highest, mixed
        for half in range(2):
            total = pltpu.roll(sums[half], HEAD_DIM, 1)
            parts.append(sums[half] / total)
            totals.append(tops[half] + jnp.log2(total))
        mixed = jnp.where(in_half(parts[0].shape, 0), parts[0], parts[1]).astype(BF16)
        limit = jnp.where(image == 0, 0, scalars[17]) - base
        row_mine = lax.broadcasted_iota(jnp.int32, mixed.shape, 0) >= limit
        lane_mine = lax.broadcasted_iota(jnp.int32, (1, TILE), 1) >= limit
        out[spot, :] = jnp.where(row_mine, mixed, out[spot, :])
        store_logs(logs, spot, totals, lane_mine)
        return carry

    lax.fori_loop(0, count, visit, 0)


def cross_forward(pair, scalars, q, keys_values, images):
    count, inner = q.shape
    pairs = inner // PAIR
    memory_rows = keys_values.shape[0] // images

    def part(which):
        return pl.BlockSpec((memory_rows, PAIR), lambda i, sc: (i, which * pairs + pair))

    return pl.pallas_call(
        cross_forward_kernel,
        grid_spec=pltpu.PrefetchScalarGridSpec(
            num_scalar_prefetch=1,
            grid=(images,),
            in_specs=[
                pl.BlockSpec((count, PAIR), lambda i, sc: (0, pair)),
                part(0),
                part(1),
            ],
            out_specs=[whole((count, PAIR)), whole((8, count))],
        ),
        out_shape=[pltpu.HBM((count, PAIR), BF16), pltpu.HBM((8, count), F32)],
        compiler_params=params(),
        cost_estimate=cost(20 * count * memory_rows * PAIR, 8 * memory_rows * PAIR),
    )(scalars, *pin(q, keys_values, keys_values))


def cross_backward_kernel(
    image, scalars, q, k, v, grad, logs, deltas, old, dq, dk, dv, key_sum, value_sum
):
    first, count = visits_of(jnp.int32(image), scalars)
    if image:
        dq[...] = old[...]

    def visit(i, fresh):
        base = pl.multiple_of((first + i) * TILE, TILE)
        spot = pl.ds(base, TILE)
        queries = q[spot, :]
        grads = grad[spot, :]
        keys = k[...]
        values = v[...]
        limit = scalars[17] - base
        lane_mine = (lax.broadcasted_iota(jnp.int32, (1, TILE), 1) >= limit) == (image == 1)
        parts = []
        for half in range(2):
            one_query = only_half(queries, half)
            one_grad = only_half(grads, half)
            log = jnp.where(lane_mine, logs[half : half + 1, spot], HIDE)
            scores = dot(keys, one_query, NT)
            weights = jnp.exp2(scores * EXP2_SCALE - log)
            slopes = dot(values, one_grad, NT)
            pushed = (weights * (slopes - deltas[half : half + 1, spot])).astype(BF16)
            value_part = dot(weights.astype(BF16), one_grad, NN)
            key_part = dot(pushed, one_query, NN)
            if fresh and half == 0:
                value_sum[...] = value_part
                key_sum[...] = key_part
            else:
                value_sum[...] += value_part
                key_sum[...] += key_part
            parts.append(dot(pushed, keys, TN))
        grad_query = (
            jnp.where(in_half(parts[0].shape, 0), parts[0], parts[1]) * SCALE
        ).astype(BF16)
        if image:
            row_mine = lax.broadcasted_iota(jnp.int32, grad_query.shape, 0) >= limit
            grad_query = jnp.where(row_mine, grad_query, dq[spot, :])
        dq[spot, :] = grad_query

    def later(i, carry):
        visit(i, False)
        return carry

    visit(0, True)
    lax.fori_loop(1, count, later, 0)
    dk[...] = (key_sum[...] * SCALE).astype(BF16)
    dv[...] = value_sum[...].astype(BF16)


def cross_backward(image, scalars, q, keys_values, grad, logs, deltas, images, old):
    count, inner = q.shape
    pairs = inner // PAIR
    memory_rows = keys_values.shape[0] // images
    token_spec = pl.BlockSpec((count, PAIR), lambda p, sc: (0, p))
    line = pl.BlockSpec((8, count), lambda p, sc: (p, 0))
    result = pl.BlockSpec((memory_rows, PAIR), lambda p, sc: (0, p))

    def part(which):
        return pl.BlockSpec((memory_rows, PAIR), lambda p, sc: (image, which * pairs + p))

    def first_kernel(scalars, q, k, v, grad, logs, deltas, *rest):
        cross_backward_kernel(image, scalars, q, k, v, grad, logs, deltas, None, *rest)

    def second_kernel(*refs):
        cross_backward_kernel(image, *refs)

    extra = [old] if image else []
    return pl.pallas_call(
        second_kernel if image else first_kernel,
        grid_spec=pltpu.PrefetchScalarGridSpec(
            num_scalar_prefetch=1,
            grid=(pairs,),
            in_specs=[token_spec, part(0), part(1), token_spec, line, line]
            + [token_spec] * len(extra),
            out_specs=[token_spec, result, result],
            scratch_shapes=[pltpu.VMEM((memory_rows, PAIR), F32)] * 2,
        ),
        out_shape=[
            pltpu.HBM((count, inner), BF16),
            pltpu.HBM((memory_rows, inner), BF16),
            pltpu.HBM((memory_rows, inner), BF16),
        ],
        compiler_params=params(32),
        cost_estimate=cost(25 * count * memory_rows * inner, 8 * memory_rows * inner),
    )(scalars, *pin(q, keys_values, keys_values, grad), logs, deltas, *pin(*extra))


def put_rows(places, product, keep, send, span=slice(None)):
    height = product.shape[0] // 4
    for i, ref in enumerate((keep, keep, send, send)):
        start = pl.multiple_of(places[i] * height, 16)
        ref[i % 2, 0:height, span] = product[pl.ds(start, height), :].astype(BF16)


def memory_back_kernel(
    columns, last, places, memory, dk, dv, w0, w1, w2, w3, *refs
):
    if last:
        before, keep_part, send_part, keep, send, weight, total, sems = refs
    else:
        keep_part, send_part, send_more, total_out, weight, total, sems = refs
    inner = dk.shape[1]

    @pl.when(pl.program_id(0) == 0)
    def _():
        copies = fetch((w0, w1, w2, w3), places, columns, weight, sems)
        start_all(copies)
        if last:
            total[...] = before[...]
        else:
            total[...] = jnp.zeros_like(total)
        wait_all(copies)

    both = jnp.concatenate([dk[...], dv[...]], axis=1)
    product = dot(both, weight[...], NT).astype(BF16)
    lower, upper = product[:, :inner], product[:, inner:]
    side = places[4]
    leave = jnp.where(side == 0, upper, lower)
    if last:
        send_part[...] = leave
    else:

        @pl.when(pl.program_id(0) < pl.num_programs(0) // 2)
        def _():
            send_part[...] = leave

        @pl.when(pl.program_id(0) >= pl.num_programs(0) // 2)
        def _():
            send_more[...] = leave

    keep_part[...] = jnp.where(side == 0, lower, upper)
    total[...] += dot(memory[...], both, TN)

    @pl.when(pl.program_id(0) == pl.num_programs(0) - 1)
    def _():
        if last:
            put_rows(places, total, keep, send)
        else:
            total_out[...] = total[...]


def memory_back(places, memory, dk, dv, pieces, columns, image, before, spare):
    count, inner = dk.shape
    width = memory.shape[1]
    steps = count // BACK_TILE
    last = before is not None
    ranks = pltpu.HBM((2, width // 4, spare + 2 * inner), BF16)
    rank_spec = pl.BlockSpec((2, width // 4, 2 * inner), lambda t: (0, 0, 0))

    def kernel(*refs):
        memory_back_kernel(columns, last, *refs)

    return pl.pallas_call(
        kernel,
        grid=(steps,),
        in_specs=[
            SCALARS,
            pl.BlockSpec((BACK_TILE, width), lambda t: (image * steps + t, 0)),
            rows(inner, BACK_TILE),
            rows(inner, BACK_TILE),
        ]
        + [ANY] * 4
        + ([whole((width, 2 * inner))] if last else []),
        out_specs=[rows(inner, BACK_TILE)]
        + (
            [rows(inner, BACK_TILE), rank_spec, rank_spec]
            if last
            else [
                pl.BlockSpec((BACK_TILE, inner), lambda t: (jnp.minimum(t, steps // 2 - 1), 0)),
                pl.BlockSpec((BACK_TILE, inner), lambda t: (jnp.maximum(t - steps // 2, 0), 0)),
                whole((width, 2 * inner)),
            ]
        ),
        out_shape=[pltpu.HBM((count, inner), BF16)]
        + (
            [pltpu.HBM((count, inner), BF16), ranks, ranks]
            if last
            else [
                pltpu.HBM((count // 2, inner), BF16),
                pltpu.HBM((count // 2, inner), BF16),
                shape_of((width, 2 * inner), F32),
            ]
        ),
        scratch_shapes=[
            pltpu.VMEM((width, 2 * inner), BF16),
            pltpu.VMEM((width, 2 * inner), F32),
            pltpu.SemaphoreType.DMA((4,)),
        ],
        compiler_params=params(),
        cost_estimate=cost(8 * count * width * inner, 8 * count * width),
    )(places, *pin(memory, dk, dv), *pieces, *([before] if last else []))


def weight_grads_kernel(plan, spans, places, left_refs, right_refs, keep, send, scratch):
    left_holds = scratch[: len(left_refs)]
    right_holds = scratch[len(left_refs) : -3]
    turned, product, sems = scratch[-3:]
    step = pl.program_id(0)
    lefts = [
        pltpu.make_async_copy(ref, hold, sems.at[i])
        for i, (ref, hold) in enumerate(zip(left_refs, left_holds))
    ]
    rights = [
        pltpu.make_async_copy(ref, hold, sems.at[len(left_refs) + i])
        for i, (ref, hold) in enumerate(zip(right_refs, right_holds))
    ]
    for at, (left, group) in enumerate(plan):
        fresh = at == 0 or plan[at - 1][0] != left

        @pl.when(step == at)
        def _():
            if at == 0:
                lefts[left].start()
                for g in group:
                    rights[g].start()
            if fresh:
                lefts[left].wait()
            if at == 0:
                begun = {left}
                for one, others in plan[1:]:
                    if one not in begun:
                        lefts[one].start()
                        begun.add(one)
                    for g in others:
                        rights[g].start()
            if fresh:
                turned[...] = left_holds[left][...].T
            for g in group:
                rights[g].wait()
            right = join([right_holds[g] for g in group])
            columns = right.shape[1]
            product[:, 0:columns] = dot(turned[...], right, NN)
            put_rows(places, product.at[:, 0:columns], keep, send, spans[at])


def join(refs):
    values = [ref[...] for ref in refs]
    return values[0] if len(values) == 1 else jnp.concatenate(values, axis=1)


def flatten(groups):
    flat, sizes = [], []
    for group in groups:
        group = group if isinstance(group, (list, tuple)) else [group]
        flat += list(group)
        sizes.append(len(group))
    return flat, sizes


def weight_grads(places, lefts, rights, plan, into=(), first=0):
    count, width = lefts[0].shape
    flat, sizes = flatten(rights)
    groups, at = [], 0
    for size in sizes:
        groups.append(list(range(at, at + size)))
        at += size
    plan = [(left, [f for g in group for f in groups[g]]) for left, group in plan]
    columns = [sum(flat[f].shape[1] for f in group) for _, group in plan]
    step_columns = columns[0]
    share = width // 4
    total = sum(columns) + first * step_columns
    even = len(set(columns)) == 1
    spans = [
        slice(0, step_columns) if even else slice(sum(columns[:at]), sum(columns[: at + 1]))
        for at in range(len(plan))
    ]
    extra = list(into)
    def kernel(places, *refs):
        lefts_end = len(lefts)
        rights_end = lefts_end + len(flat)
        weight_grads_kernel(
            plan,
            spans,
            places,
            refs[:lefts_end],
            refs[lefts_end:rights_end],
            *refs[rights_end + len(extra) : rights_end + len(extra) + 2],
            refs[rights_end + len(extra) + 2 :],
        )

    start = 1 + len(lefts) + len(flat)
    return pl.pallas_call(
        kernel,
        grid=(len(plan),),
        in_specs=[SCALARS]
        + [ANY] * (len(lefts) + len(flat) + len(extra)),
        out_specs=[
            pl.BlockSpec((2, share, step_columns), lambda t: (0, 0, t + first))
            if even
            else whole((2, share, total))
        ]
        * 2,
        out_shape=[pltpu.HBM((2, share, total), BF16)] * 2,
        input_output_aliases={start: 0, start + 1: 1} if extra else {},
        scratch_shapes=[pltpu.VMEM(array.shape, array.dtype) for array in list(lefts) + flat]
        + [
            pltpu.VMEM((width, count), BF16),
            pltpu.VMEM((width, max(columns)), F32),
            pltpu.SemaphoreType.DMA((len(lefts) + len(flat),)),
        ],
        compiler_params=params(32),
        cost_estimate=cost(
            2 * count * width * sum(columns), 4 * count * width * len(plan)
        ),
    )(places, *pin(*lefts, *flat), *extra)


def middle_kernel(plan, parts, places, x, gain, *refs):
    mine, theirs, refs = refs[:parts], refs[parts : 2 * parts], refs[2 * parts :]
    pieces, (h1, n2, cq, out_mine, out_theirs, query, sems) = refs[:8], refs[8:]

    @pl.when(pl.program_id(0) == 0)
    def _():
        copies = (
            fetch(pieces[:4], places, plan[0], out_mine, sems, 0)
            + fetch(pieces[4:], places, plan[1], out_theirs, sems, 4)
            + fetch(pieces[:4], places, plan[2], query, sems, 8)
        )
        start_all(copies)
        wait_all(copies)

    values = (
        x[...].astype(F32)
        + dot(join(mine), out_mine[...], NT)
        + dot(join(theirs), out_theirs[...], NT)
    )
    h1[...] = values.astype(BF16)
    normed = (values * inverse_rms(values) * gain[...]).astype(BF16)
    n2[...] = normed
    cq[...] = dot(normed, query[...], NN).astype(BF16)


def middle_step(places, x, mine, theirs, gain, pieces, pieces_theirs, plan):
    count, width = x.shape
    half = sum(part.shape[1] for part in mine)

    def kernel(*refs):
        middle_kernel(plan, len(mine), *refs)

    return pl.pallas_call(
        kernel,
        grid=(count // ROWS,),
        in_specs=[SCALARS, rows(width), whole((1, width))]
        + [rows(PAIR)] * (2 * len(mine))
        + [ANY] * 8,
        out_specs=[rows(width), rows(width), rows(half)],
        out_shape=[
            pltpu.HBM((count, width), BF16),
            pltpu.HBM((count, width), BF16),
            pltpu.HBM((count, half), BF16),
        ],
        scratch_shapes=[pltpu.VMEM((width, half), BF16)] * 3 + [pltpu.SemaphoreType.DMA((12,))],
        compiler_params=params(),
        cost_estimate=cost(6 * count * width * half, 12 * count * width),
    )(places, *pin(x), gain, *pin(*mine), *theirs, *pieces, *pieces_theirs)


def head_sums(left, right):
    product = left.astype(F32) * right.astype(F32)
    width = product.shape[1]
    high = product.astype(BF16)
    low = (product - high.astype(F32)).astype(BF16)
    height = 8 * (width // PAIR)
    line = lax.broadcasted_iota(jnp.int32, (height, width), 0)
    head = lax.broadcasted_iota(jnp.int32, (height, width), 1) // HEAD_DIM
    choose = (
        ((line // 8) * 2 + line % 8 == head) & (line % 8 < 2)
    ).astype(F32).astype(BF16)
    return dot(choose, high, NT) + dot(choose, low, NT)


CHUNK = 512


def units_kernel(plan, parts, places, h1, gain, gy, *refs):
    mine, theirs, refs = refs[:parts], refs[parts : 2 * parts], refs[2 * parts :]
    late, refs = refs[0], refs[1:]
    (
        output,
        n3,
        hidden,
        grad_gate,
        grad_up,
        e2,
        dc,
        deltas,
        gain_grad,
        out_mine,
        out_theirs,
        units_mine,
        units_theirs,
        sems,
    ) = refs
    step = pl.program_id(0)

    side = places[4]
    out_copies = [
        fetch_half(late, side, plan[0], out_mine, sems.at[0]),
        fetch_half(late, 1 - side, plan[0], out_theirs, sems.at[1]),
    ]
    mine_copy = fetch_half(late, side, plan[1], units_mine, sems.at[2])
    theirs_copy = fetch_half(late, 1 - side, plan[1], units_theirs, sems.at[3])

    @pl.when(step == 0)
    def _():
        start_all(out_copies + [mine_copy, theirs_copy])
        gain_grad[...] = jnp.zeros_like(gain_grad)
        wait_all(out_copies)

    crossed_mine = join(mine)
    values = (
        h1[...].astype(F32)
        + dot(crossed_mine, out_mine[...], NT)
        + dot(join(theirs), out_theirs[...], NT)
    )
    normed = (values * inverse_rms(values) * gain[...]).astype(BF16)
    n3[...] = normed
    upstream = gy[...]
    mixed = jnp.zeros_like(values)
    back = jnp.zeros_like(values)
    unit = units_mine.shape[1] // 3
    for own in (True, False):
        weight = units_mine if own else units_theirs

        @pl.when(step == 0)
        def _():
            (mine_copy if own else theirs_copy).wait()

        for start in range(0, unit, CHUNK):
            gate_weight = weight[:, start : start + CHUNK]
            up_weight = weight[:, unit + start : unit + start + CHUNK]
            down_weight = weight[:, 2 * unit + start : 2 * unit + start + CHUNK]
            gate = dot(normed, gate_weight, NN)
            up = dot(normed, up_weight, NN)
            pushed = dot(upstream, down_weight, NN)
            square = gate * gate
            bend = jnp.tanh(ROOT_TWO_OVER_PI * gate * (1.0 + CUBIC * square))
            lift = 0.5 * (1.0 + bend)
            gelu = gate * lift
            slope = lift + (0.5 * ROOT_TWO_OVER_PI) * gate * (1.0 - bend * bend) * (
                1.0 + (3.0 * CUBIC) * square
            )
            units = (gelu * up).astype(BF16)
            push_gate = (pushed * up * slope).astype(BF16)
            push_up = (pushed * gelu).astype(BF16)
            mixed = mixed + dot(units, down_weight, NT)
            back = back + dot(push_gate, gate_weight, NT) + dot(push_up, up_weight, NT)
            if own:
                hidden[:, start : start + CHUNK] = units
                grad_gate[:, start : start + CHUNK] = push_gate
                grad_up[:, start : start + CHUNK] = push_up
    output[...] = (values + mixed).astype(BF16)
    grad, gain_part = norm_back(values, gain[...], back)
    low = (upstream.astype(F32) + grad).astype(BF16)
    e2[...] = low
    crossed = dot(low, out_mine[...], NN).astype(BF16)
    dc[...] = crossed
    deltas[...] = head_sums(crossed, crossed_mine)
    gain_grad[0:1, :] += gain_part


def units_step(places, h1, mine, theirs, gain, gy, late, plan):
    count, width = h1.shape
    half = sum(part.shape[1] for part in mine)
    unit = (plan[1].stop - plan[1].start) // 3
    lines = 8 * (half // PAIR)

    def kernel(*refs):
        units_kernel(plan, len(mine), *refs)

    return pl.pallas_call(
        kernel,
        grid=(count // ROWS,),
        in_specs=[
            SCALARS,
            rows(width),
            whole((1, width)),
            rows(width),
        ]
        + [rows(PAIR)] * (2 * len(mine))
        + [ANY],
        out_specs=[
            rows(width),
            rows(width),
            rows(unit),
            rows(unit),
            rows(unit),
            rows(width),
            rows(half),
            pl.BlockSpec((lines, ROWS), lambda t: (0, t)),
            whole((8, width)),
        ],
        out_shape=[
            pltpu.HBM((count, width), BF16),
            pltpu.HBM((count, width), BF16),
            pltpu.HBM((count, unit), BF16),
            pltpu.HBM((count, unit), BF16),
            pltpu.HBM((count, unit), BF16),
            pltpu.HBM((count, width), BF16),
            pltpu.HBM((count, half), BF16),
            pltpu.HBM((lines, count), F32),
            shape_of((8, width), F32),
        ],
        scratch_shapes=[pltpu.VMEM((width, half), BF16)] * 2
        + [pltpu.VMEM((width, 3 * unit), BF16)] * 2
        + [pltpu.SemaphoreType.DMA((4,))],
        compiler_params=params(58),
        cost_estimate=cost(30 * count * width * unit, 30 * count * width),
    )(places, *pin(h1), gain, *pin(gy, *mine), *theirs, *pin(late))


def turn_kernel(plan, parts, places, e2, h1, mine, theirs, gain, *refs):
    attended, refs = refs[:parts], refs[parts:]
    pieces, refs = refs[:4], refs[4:]
    late, e1, da, deltas, gain_grad, query_mine, query_theirs, out_mine, sems = refs

    @pl.when(pl.program_id(0) == 0)
    def _():
        copies = (
            fetch(pieces, places, plan[0], out_mine, sems, 0)
            + fetch(pieces, places, plan[1], query_mine, sems, 4)
            + [fetch_half(late, 1 - places[4], plan[2], query_theirs, sems.at[8])]
        )
        start_all(copies)
        gain_grad[...] = jnp.zeros_like(gain_grad)
        wait_all(copies)

    back = dot(mine[...], query_mine[...], NT) + dot(theirs[...], query_theirs[...], NT)
    grad, gain_part = norm_back(h1[...].astype(F32), gain[...], back)
    low = (e2[...].astype(F32) + grad).astype(BF16)
    e1[...] = low
    pushed = dot(low, out_mine[...], NN).astype(BF16)
    da[...] = pushed
    deltas[...] = head_sums(pushed, join(attended))
    gain_grad[0:1, :] += gain_part


def turn_step(places, e2, h1, mine, theirs, gain, attended, pieces, late, plan):
    count, width = h1.shape
    half = mine.shape[1]
    lines = 8 * (half // PAIR)

    def kernel(*refs):
        turn_kernel(plan, len(attended), *refs)

    return pl.pallas_call(
        kernel,
        grid=(count // ROWS,),
        in_specs=[
            SCALARS,
            rows(width),
            rows(width),
            rows(half),
            rows(half),
            whole((1, width)),
        ]
        + [rows(PAIR)] * len(attended)
        + [ANY] * 5,
        out_specs=[
            rows(width),
            rows(half),
            pl.BlockSpec((lines, ROWS), lambda t: (0, t)),
            whole((8, width)),
        ],
        out_shape=[
            pltpu.HBM((count, width), BF16),
            shape_of((count, half), BF16),
            shape_of((lines, count), F32),
            shape_of((8, width), F32),
        ],
        scratch_shapes=[pltpu.VMEM((width, half), BF16)] * 3 + [pltpu.SemaphoreType.DMA((9,))],
        compiler_params=params(),
        cost_estimate=cost(6 * count * width * half, 16 * count * width),
    )(places, *pin(e2, h1, mine), theirs, gain, *pin(*attended), *pieces, *pin(late))


def partial_kernel(parts, places, x, n1, second, third, *refs):
    part_refs, refs = refs[:parts], refs[parts:]
    w0, w1, w2, w3, out, keep, send, weight, total, gain_grad, sems = refs
    step = pl.program_id(0)

    @pl.when(step == 0)
    def _():
        copies = fetch((w0, w1, w2, w3), places, slice(0, weight.shape[1]), weight, sems)
        start_all(copies)
        gain_grad[...] = jnp.zeros_like(gain_grad)
        total[...] = jnp.zeros_like(total)
        wait_all(copies)

    back = dot(join(part_refs), weight[...], NT)
    out[...] = back.astype(BF16)
    values = x[...].astype(F32)
    gain_grad[0:1, :] += jnp.sum(back * values * inverse_rms(values), axis=0, keepdims=True)
    last = join([part_refs[i * (parts // 3) + parts // 3 - 1] for i in range(3)])
    total[...] += dot(n1[...], last, TN)

    @pl.when(step == pl.num_programs(0) - 1)
    def _():
        put_rows(places, total, keep, send)
        height = total.shape[0] // 4
        lines = jnp.concatenate(
            [
                gain_grad[0:1, :],
                second[0:1, :],
                third[0:1, :],
                jnp.zeros((13, gain_grad.shape[1]), F32),
            ],
            axis=0,
        )
        shares = [lines[:, w * height : (w + 1) * height] for w in range(4)]
        fill = jnp.zeros((16, total.shape[1] - height), F32)
        for i, ref in enumerate((keep, keep, send, send)):
            share = shares[0]
            for w in range(1, 4):
                share = jnp.where(places[i] == w, shares[w], share)
            ref[i % 2, height : height + 16, :] = jnp.concatenate([share, fill], axis=1).astype(
                BF16
            )


def partial_step(places, parts, x, n1, second, third, pieces):
    count, width = x.shape
    inner = sum(part.shape[1] for part in parts)
    ranks = (2, width // 4 + 16, 3 * PAIR)

    def kernel(*refs):
        partial_kernel(len(parts), *refs)

    return pl.pallas_call(
        kernel,
        grid=(count // ROWS,),
        in_specs=[SCALARS, rows(width), rows(width), whole((8, width)), whole((8, width))]
        + [rows(PAIR)] * len(parts)
        + [ANY] * 4,
        out_specs=[rows(width), whole(ranks), whole(ranks)],
        out_shape=[
            pltpu.HBM((count, width), BF16),
            shape_of(ranks, BF16),
            shape_of(ranks, BF16),
        ],
        scratch_shapes=[
            pltpu.VMEM((width, inner), BF16),
            pltpu.VMEM((width, 3 * PAIR), F32),
            pltpu.VMEM((8, width), F32),
            pltpu.SemaphoreType.DMA((4,)),
        ],
        compiler_params=params(),
        cost_estimate=cost(2 * count * width * (inner + 3 * PAIR), 8 * count * width),
    )(places, *pin(x, n1), second, third, *pin(*parts), *pieces)


def last_kernel(pos, e1, x, mine, theirs, gain, out, held):
    step = pl.program_id(0)
    half = pl.num_programs(0) // 2
    size = e1.shape[0]

    @pl.when(step < half)
    def _():
        back = mine[...].astype(F32) + theirs[...].astype(F32)
        grad, _ = norm_back(x[...].astype(F32), gain[...], back)
        held[pl.ds(pl.multiple_of(step * size, size), size), :] = (
            e1[...].astype(F32) + grad
        ).astype(BF16)

    @pl.when(step >= half)
    def _():
        onehot = (
            lax.broadcasted_iota(jnp.int32, (held.shape[0], size), 0) == pos[0:1, :]
        ).astype(F32).astype(BF16)
        out[...] = dot(onehot, held[...], TN).astype(BF16)


def last_step(pos, e1, x, mine, theirs, gain):
    count, width = x.shape
    steps = count // TILE

    def early(t):
        return (jnp.minimum(t, steps - 1), 0)

    def late(t):
        return jnp.maximum(t - steps, 0)

    tile = pl.BlockSpec((TILE, width), early)
    return pl.pallas_call(
        last_kernel,
        grid=(2 * steps,),
        in_specs=[pl.BlockSpec((8, TILE), lambda t: (0, late(t)))]
        + [tile] * 4
        + [whole((1, width))],
        out_specs=pl.BlockSpec((TILE, width), lambda t: (late(t), 0)),
        out_shape=shape_of((count, width), BF16),
        scratch_shapes=[pltpu.VMEM((count, width), BF16)],
        compiler_params=params(),
        cost_estimate=cost(2 * count * count * width, 12 * count * width),
    )(pos, *pin(e1, x, mine), theirs, gain)


def swap(values, axis, distance):
    size = lax.axis_size(axis)
    return lax.ppermute(values, axis, [(i, i ^ distance) for i in range(size)])


def after(values, *others):
    return lax.optimization_barrier((values,) + others)[0]


def gather_all(values):
    return lax.all_gather(values, ("narrow", "wide"), axis=0, tiled=True).reshape(
        lax.axis_size("narrow"), -1, values.shape[1]
    )


def sum_wide(values):
    return lax.psum_scatter(values, "wide", scatter_dimension=0, tiled=True)


def add(left, right):
    return (left.astype(F32) + right.astype(F32)).astype(BF16)


def add_pair(keep, got):
    return add(keep[0], got[0]), add(keep[1], got[1])


def line_inner():
    place = lax.axis_index("dp")
    return (place == 1) | (place == 2)


def line_first(values):
    if lax.axis_size("dp") != 4:
        return lax.psum(values, "dp")
    got = lax.ppermute(values, "dp", [(0, 1), (3, 2)])
    return jnp.where(line_inner(), add(values, got), values)


def line_second(values):
    if lax.axis_size("dp") != 4:
        return values
    return add(values, lax.ppermute(values, "dp", [(1, 2), (2, 1)]))


def line_third(values, *others):
    if lax.axis_size("dp") != 4:
        return values
    got = after(lax.ppermute(values, "dp", [(1, 0), (2, 3)]), *others)
    return jnp.where(line_inner(), values, got)


def local(
    tokens,
    memory,
    cotangent,
    norm1_gain,
    norm2_gain,
    norm3_gain,
    q_weight,
    k_weight,
    v_weight,
    o_weight,
    cross_q,
    cross_k,
    cross_v,
    cross_o,
    gate_weight,
    up_weight,
    down_weight,
    segment_ids,
    block_ids,
    image_table,
):
    width = tokens.shape[1]
    share = q_weight.shape[0]
    inner = q_weight.shape[1]
    unit = gate_weight.shape[1]
    images = memory.shape[0]
    flat_memory = memory.reshape(-1, width)
    place = lax.axis_index("wide")
    side = lax.axis_index("narrow")
    places = jnp.stack([place, place ^ 2, place ^ 1, place ^ 3, side]).astype(jnp.int32)

    gains = jnp.stack([norm1_gain, norm2_gain, norm3_gain])
    gains = jnp.pad(gains, ((0, 13), (0, 3 * inner - share)))
    early = jnp.concatenate(
        [jnp.concatenate([q_weight, k_weight, v_weight], axis=1), gains], axis=0
    )
    early_x = swap(early, "wide", 2)
    early_core = swap(early, "wide", 1)
    early_pieces = (early, early_x, early_core, swap(early_x, "wide", 1))
    lines = jnp.stack([piece[share : share + 3, :share] for piece in early_pieces])
    lines = lines.astype(F32)
    order = [
        jnp.sum(jnp.where((places[:4] == w)[:, None, None], lines, 0.0), axis=0)
        for w in range(4)
    ]
    all_gains = jnp.concatenate(order, axis=1)[:, None, :]

    mid = jnp.concatenate([cross_k, cross_v, cross_q, o_weight], axis=1)
    memory_columns = slice(0, 2 * inner)
    query_columns = slice(2 * inner, 3 * inner)
    out_columns = slice(3 * inner, 4 * inner)
    mid_x = swap(after(mid, early_x), "wide", 2)
    mid_core = swap(mid, "wide", 1)
    out_y = swap(o_weight, "narrow", 1)
    late = jnp.concatenate([cross_q, cross_o, gate_weight, up_weight, down_weight], axis=1)
    late_query_columns = slice(0, inner)
    late_columns = (slice(inner, 2 * inner), slice(2 * inner, 2 * inner + 3 * unit))

    x, row_ids, col_ids, pos, scalars = order_rows(
        segment_ids, block_ids, image_table, after(tokens, early_core, out_y)
    )
    late = gather_all(after(late, early_x, x))
    n1, qkv = norm_project(places, x, all_gains[0], early_pieces)
    pairs = inner // PAIR
    self_parts = [self_forward(0, after(qkv, mid_core), row_ids, col_ids)]
    out_yx = after(swap(out_y, "wide", 2), self_parts[0][0])
    out_pieces = (out_y, out_yx, swap(out_y, "wide", 1), swap(out_yx, "wide", 1))
    for pair in range(1, pairs):
        waits = out_pieces if pair == pairs - 1 else ()
        self_parts.append(
            self_forward(pair, after(qkv, self_parts[-1][0], *waits), row_ids, col_ids)
        )
    mid_x = after(mid_x, self_parts[-1][0])
    mid_pieces = (mid, mid_x, mid_core, swap(mid_x, "wide", 1))
    gy = order_more(pos, after(cotangent, self_parts[-1][0]))
    attended_theirs = [swap(part[0], "narrow", 1) for part in self_parts]
    attended = [part[0] for part in self_parts]
    keys_values = project_memory(
        places,
        after(flat_memory, gy, attended_theirs[0]),
        mid_pieces,
        memory_columns,
    )
    h1, n2, cq = middle_step(
        places,
        after(x, keys_values),
        attended,
        attended_theirs,
        all_gains[1],
        mid_pieces,
        out_pieces,
        (out_columns, slice(0, inner), query_columns),
    )
    cross_parts = [cross_forward(0, scalars, cq, keys_values, images)]
    crossed_theirs = []
    for pair in range(1, pairs):
        previous = [cross_parts[-1][0]] + crossed_theirs
        crossed_theirs.append(swap(cross_parts[-1][0], "narrow", 1))
        cross_parts.append(
            cross_forward(pair, scalars, after(cq, *previous), keys_values, images)
        )
    crossed = [part[0] for part in cross_parts]
    crossed_theirs.append(swap(crossed[-1], "narrow", 1))
    cross_logs = jnp.concatenate([part[1] for part in cross_parts], axis=0)
    (
        output,
        n3,
        hidden,
        grad_gate,
        grad_up,
        e2,
        dc,
        cross_deltas,
        third_gain,
    ) = units_step(
        places,
        h1,
        crossed,
        crossed_theirs,
        all_gains[2],
        gy,
        late,
        late_columns,
    )

    unit_keep, unit_send = weight_grads(
        places, (n3, gy), (grad_gate, grad_up, hidden), ((0, (0,)), (0, (1,)), (1, (2,)))
    )
    unit_stay, unit_leave = add_pair(unit_keep, swap(unit_send, "wide", 1))
    dcq, dck, dcv = cross_backward(
        0,
        scalars,
        cq,
        keys_values,
        after(dc, unit_leave),
        cross_logs,
        cross_deltas,
        images,
        None,
    )
    unit_part = add(unit_stay, swap(unit_leave, "wide", 2))
    keep0, send0, more0, total = memory_back(
        places,
        flat_memory,
        after(dck, unit_part),
        dcv,
        mid_pieces,
        memory_columns,
        0,
        None,
        0,
    )
    unit_sum = lax.psum(unit_part, "dp")
    dcq, dck, dcv = cross_backward(
        1,
        scalars,
        cq,
        keys_values,
        after(dc, send0),
        cross_logs,
        cross_deltas,
        images,
        dcq,
    )
    dcq_theirs = swap(dcq, "narrow", 1)
    got0 = swap(send0, "narrow", 1)
    got_more = swap(after(more0, dcq), "narrow", 1)
    keep1, send1, cross_keep, cross_send = memory_back(
        places,
        flat_memory,
        after(dck, got0),
        dcv,
        mid_pieces,
        memory_columns,
        1,
        total,
        2 * inner,
    )
    cross_keep, cross_send = weight_grads(
        places,
        (after(n2, send1), e2),
        (dcq, crossed),
        ((0, (0,)), (1, (1,))),
        into=(cross_keep, cross_send),
        first=2,
    )
    e1, da, self_deltas, second_gain = turn_step(
        places,
        e2,
        h1,
        after(dcq, cross_send, unit_sum),
        dcq_theirs,
        all_gains[1],
        attended,
        mid_pieces,
        late,
        (out_columns, query_columns, late_query_columns),
    )
    got1 = swap(after(send1, dcq_theirs, got0), "narrow", 1)
    cross_stay, cross_leave = add_pair(cross_keep, swap(cross_send, "wide", 1))
    da = after(da, cross_leave)
    back = []
    for pair in range(pairs):
        ready = after(da, *[part[0] for part in back])
        if pair == pairs - 1:
            early_back = list(back)
            self_keep, self_send = weight_grads(
                places,
                (after(n1, back[-1][0]), e1),
                [[part[i] for part in early_back] for i in range(3)] + [attended],
                ((0, (0, 1, 2)), (1, (3,))),
            )
            cross_part = add(cross_stay, swap(cross_leave, "wide", 2))
            ready = after(ready, cross_part, self_send)
            cross_part = line_first(cross_part)
        back.append(
            self_backward(
                pair, qkv, ready, self_parts[pair][1], self_deltas, row_ids, col_ids
            )
        )
    dq, dk, dv = [[part[i] for part in back] for i in range(3)]
    self_stay, self_leave = add_pair(self_keep, swap(self_send, "wide", 1))
    self_part = add(self_stay, swap(self_leave, "wide", 2))
    dn1, last_keep, last_send = partial_step(
        places,
        dq + dk + dv,
        after(x, self_leave),
        n1,
        second_gain,
        third_gain,
        early_pieces,
    )
    dn1_theirs = swap(dn1, "narrow", 1)
    memory0 = add(after(keep0, dn1), jnp.concatenate([got0, got_more]))
    memory1 = add(after(keep1, dn1), got1)
    last_stay, last_leave = add_pair(last_keep, swap(last_send, "wide", 1))
    last_part = add(last_stay, swap(last_leave, "wide", 2))
    output = restore_rows(pos, after(output, last_send, self_part))
    tokens_grad = last_step(pos, e1, x, dn1, dn1_theirs, all_gains[0])
    memory_grad = jnp.stack([after(memory0, self_part), memory1])
    cross_sum = line_third(line_second(cross_part), tokens_grad)
    self_second = line_second(line_first(self_part))
    self_sum = line_third(self_second, tokens_grad)
    last_sum = line_third(line_second(line_first(last_part)))
    gain_sums = last_sum[share:, :share].astype(F32)
    first_gain = gain_sums[0] + swap(after(gain_sums, self_second), "narrow", 1)[0]

    def grads(array, size, count):
        return [array[:share, i * size : (i + 1) * size].astype(F32) for i in range(count)]

    gate_grad, up_grad, down_grad = grads(after(unit_sum, self_part), unit, 3)
    cross_k_grad, cross_v_grad, cross_q_grad, cross_o_grad = grads(cross_sum, inner, 4)
    part = inner - PAIR
    q_grad, k_grad, v_grad = [
        jnp.concatenate([most, rest], axis=1)
        for most, rest in zip(grads(self_sum, part, 3), grads(last_sum, PAIR, 3))
    ]
    o_grad = self_sum[:, 3 * part :].astype(F32)
    return (
        output,
        tokens_grad,
        memory_grad,
        first_gain,
        gain_sums[1],
        gain_sums[2],
        q_grad,
        k_grad,
        v_grad,
        o_grad,
        cross_q_grad,
        cross_k_grad,
        cross_v_grad,
        cross_o_grad,
        gate_grad,
        up_grad,
        down_grad,
    )


def solution(mesh):
    both = ("dp", "wide")
    weight = P("wide", "narrow")
    in_specs = (
        (P(both, None), P(both, None, None), P(both, None))
        + (P("wide"),) * 3
        + (weight,) * 11
        + (P(both, None),) * 3
    )
    out_specs = (
        (P(both, None), P(both, None), P(both, None, "narrow"))
        + (P("wide"),) * 3
        + (weight,) * 11
    )
    return jax.shard_map(local, mesh=mesh, in_specs=in_specs, out_specs=out_specs, check_vma=False)
```

profile of v0, /device:TPU:0, one launch (start us, length us, event | category | flops | bytes accessed | tf_op | source)
XLA Modules:
  0.0 396.8 jit_solution(12317853868043605097)
XLA Ops:
  20.9 5.8 %shard_map.323 = (bf16[1024,768]{1,0:T(8,128)(2,1)}, f32[8,1024]{1,0:T(8,128)S(1)}, f32[1024,128]{1,0:T(8,128)S(1)}, s32[8,1024]{1,0:T(8,128)S(1)}, s32[32]{0:T(128)S(1)}) custom-call(s32[1,1024]{1,0:T(1,128)S(1)} %copy-done.17, s32[1,1024]{1,0:T(1,128)S(1)} %copy-done.18, s32[1,8]{1,0:T(1,128)S(1)} %copy-done.19, bf16[1024,768]{1,0:T(8,128)(2,1)} %x.2), custom_call_target="tpu_custom_call" | custom-call | flops 6442450944 | bytes 25165824 | tf_op jit(solution)/shard_map/pallas_call | solution.py:140
  32.3 5.3 %shard_map.324 = (bf16[1024,768]{1,0:T(8,128)(2,1)}, bf16[1024,1152]{1,0:T(8,128)(2,1)S(1)}) custom-call(s32[5]{0:T(128)S(1)} %stack.65.places.refs_0_, bf16[1024,768]{1,0:T(8,128)(2,1)} %get-tuple-element.196.x.refs_1_, f32[1,768]{1,0:T(1,128)S(1)} %get-tuple-element.247.gain, bf16[208,1152]{1,0:T(8,128)(2,1)S(1)} %fusion.11.w0.refs_14_, ...), custom_call_target="tpu_custom_call" | custom-call | flops 7247757312 | bytes 22020096 | tf_op jit(solution)/shard_map/pallas_call | solution.py:259
  37.7 4.5 %shard_map.325 = (bf16[1024,128]{1,0:T(8,128)(2,1)}, f32[8,1024]{1,0:T(8,128)}) custom-call(bf16[1024,1152]{1,0:T(8,128)(2,1)S(1)} %get-tuple-element.130.q.k.v, bf16[1024,1152]{1,0:T(8,128)(2,1)S(1)} %get-tuple-element.130.q.k.v, bf16[1024,1152]{1,0:T(8,128)(2,1)S(1)} %get-tuple-element.130.q.k.v, f32[8,1024]{1,0:T(8,128)S(1)} %get-tuple-element.124.row_ids, ...), custom_call_target="tpu_custom_call" | custom-call | flops 5368709120 | bytes 4194304 | tf_op jit(solution)/shard_map/pallas_call | solution.py:351
  53.7 5.0 %collective-permute-done.9.refs_2_.refs_10_.refs_5_ = bf16[192,1536]{1,0:T(8,128)(2,1)S(1)} collective-permute-done((bf16[192,1536]{1,0:T(8,128)(2,1)S(1)}, bf16[192,1536]{1,0:T(8,128)(2,1)S(1)}, u32[]{:S(2)}, u32[]{:S(2)}) %collective-permute-start.9) | collective-permute-done | bytes 589856 | tf_op jit(solution)/shard_map/ppermute | solution.py:1203
  58.8 5.3 %shard_map.328.refs_3_.refs_1_ = bf16[1024,768]{1,0:T(8,128)(2,1)} custom-call(s32[8,1024]{1,0:T(8,128)S(1)} %get-tuple-element.120.pos, bf16[1024,768]{1,0:T(8,128)(2,1)} %values), custom_call_target="tpu_custom_call" | custom-call | flops 6442450944 | bytes 12582912 | tf_op jit(solution)/shard_map/pallas_call | solution.py:178
  64.1 9.5 %shard_map.329.k.v.refs_2_.refs_3_ = bf16[4096,768]{1,0:T(8,128)(2,1)} custom-call(s32[5]{0:T(128)S(1)} %stack.65.places.refs_0_, bf16[4096,768]{1,0:T(8,128)(2,1)} %bitcast.55, bf16[192,1536]{1,0:T(8,128)(2,1)S(1)} %constant_dynamic-update-slice_fusion.refs_1_.refs_9_.refs_4_, bf16[192,1536]{1,0:T(8,128)(2,1)S(1)} %collective-permute-done.9.refs_2_.refs_10_.refs_5_, ...), custom_call_target="tpu_custom_call" | custom-call | flops 19327352832 | bytes 50331648 | tf_op jit(solution)/shard_map/pallas_call | solution.py:292
  73.6 7.9 %shard_map.330 = (bf16[1024,768]{1,0:T(8,128)(2,1)}, bf16[1024,768]{1,0:T(8,128)(2,1)}, bf16[1024,384]{1,0:T(8,128)(2,1)}) custom-call(s32[5]{0:T(128)S(1)} %stack.65.places.refs_0_, bf16[1024,768]{1,0:T(8,128)(2,1)} %get-tuple-element.196.x.refs_1_, f32[1,768]{1,0:T(1,128)S(1)} %get-tuple-element.246.refs_2_.refs_5_, ...), custom_call_target="tpu_custom_call" | custom-call | flops 7247757312 | bytes 37748736 | tf_op jit(solution)/shard_map/pallas_call | solution.py:843
  81.6 11.1 %shard_map.331 = (bf16[1024,128]{1,0:T(8,128)(2,1)}, f32[8,1024]{1,0:T(8,128)}) custom-call(s32[32]{0:T(128)S(1)} %get-tuple-element.138.scalars.refs_0_, bf16[1024,384]{1,0:T(8,128)(2,1)} %get-tuple-element.143.q.refs_1_, bf16[4096,768]{1,0:T(8,128)(2,1)} %shard_map.329.k.v.refs_2_.refs_3_, bf16[4096,768]{1,0:T(8,128)(2,1)} %shard_map.329.k.v.refs_2_.refs_3_), custom_call_target="tpu_custom_call" | custom-call | flops 21474836480 | bytes 8388608 | tf_op jit(solution)/shard_map/pallas_call | solution.py:483
  92.7 11.1 %shard_map.332 = (bf16[1024,128]{1,0:T(8,128)(2,1)}, f32[8,1024]{1,0:T(8,128)}) custom-call(s32[32]{0:T(128)S(1)} %get-tuple-element.138.scalars.refs_0_, bf16[1024,384]{1,0:T(8,128)(2,1)} %get-tuple-element.143.q.refs_1_, bf16[4096,768]{1,0:T(8,128)(2,1)} %shard_map.329.k.v.refs_2_.refs_3_, bf16[4096,768]{1,0:T(8,128)(2,1)} %shard_map.329.k.v.refs_2_.refs_3_), custom_call_target="tpu_custom_call" | custom-call | flops 21474836480 | bytes 8388608 | tf_op jit(solution)/shard_map/pallas_call | solution.py:483
  107.7 11.1 %shard_map.333 = (bf16[1024,128]{1,0:T(8,128)(2,1)}, f32[8,1024]{1,0:T(8,128)}) custom-call(s32[32]{0:T(128)S(1)} %get-tuple-element.138.scalars.refs_0_, bf16[1024,384]{1,0:T(8,128)(2,1)} %get-tuple-element.143.q.refs_1_, bf16[4096,768]{1,0:T(8,128)(2,1)} %shard_map.329.k.v.refs_2_.refs_3_, bf16[4096,768]{1,0:T(8,128)(2,1)} %shard_map.329.k.v.refs_2_.refs_3_), custom_call_target="tpu_custom_call" | custom-call | flops 21474836480 | bytes 8388608 | tf_op jit(solution)/shard_map/pallas_call | solution.py:483
  118.8 8.1 %collective-permute-done.15.refs_9_ = bf16[1024,128]{1,0:T(8,128)(2,1)} collective-permute-done((bf16[1024,128]{1,0:T(8,128)(2,1)}, bf16[1024,128]{1,0:T(8,128)(2,1)}, u32[]{:S(2)}, u32[]{:S(2)}) %collective-permute-start.15) | collective-permute-done | bytes 262176 | tf_op jit(solution)/shard_map/ppermute | solution.py:1203
  126.9 33.0 %shard_map.334 = (bf16[1024,768]{1,0:T(8,128)(2,1)}, bf16[1024,768]{1,0:T(8,128)(2,1)}, bf16[1024,1024]{1,0:T(8,128)(2,1)}, bf16[1024,1024]{1,0:T(8,128)(2,1)}, ...) custom-call(s32[5]{0:T(128)} %copy-done.4, ...), custom_call_target="tpu_custom_call" | custom-call | flops 96636764160 | bytes 94371840 | tf_op jit(solution)/shard_map/pallas_call | solution.py:974
  160.0 10.3 %shard_map.335 = (bf16[2,192,3072]{2,1,0:T(8,128)(2,1)}, bf16[2,192,3072]{2,1,0:T(8,128)(2,1)}) custom-call(s32[5]{0:T(128)S(1)} %copy-done.5, bf16[1024,768]{1,0:T(8,128)(2,1)} %get-tuple-element.150.refs_0_, bf16[1024,768]{1,0:T(8,128)(2,1)} %shard_map.328.refs_3_.refs_1_, bf16[1024,1024]{1,0:T(8,128)(2,1)} %get-tuple-element.151.refs_2_, ...), custom_call_target="tpu_custom_call" | custom-call | flops 19327352832 | bytes 37748736 | tf_op jit(solution)/shard_map/pallas_call | solution.py:785
  170.4 4.7 %collective-permute-done.16 = bf16[2,192,3072]{2,1,0:T(8,128)(2,1)S(1)} collective-permute-done((bf16[2,192,3072]{2,1,0:T(8,128)(2,1)}, bf16[2,192,3072]{2,1,0:T(8,128)(2,1)S(1)}, u32[]{:S(2)}, u32[]{:S(2)}) %collective-permute-start.16) | collective-permute-done | bytes 2359328 | tf_op jit(solution)/shard_map/ppermute | solution.py:1203
  177.3 38.5 %shard_map.336 = (bf16[1024,384]{1,0:T(8,128)(2,1)}, bf16[2048,384]{1,0:T(8,128)(2,1)}, bf16[2048,384]{1,0:T(8,128)(2,1)}) custom-call(s32[32]{0:T(128)S(1)} %get-tuple-element.138.scalars.refs_0_, bf16[1024,384]{1,0:T(8,128)(2,1)} %get-tuple-element.143.q.refs_1_, bf16[4096,768]{1,0:T(8,128)(2,1)} %shard_map.329.k.v.refs_2_.refs_3_, ...), custom_call_target="tpu_custom_call" | custom-call | flops 80530636800 | bytes 25165824 | tf_op jit(solution)/shard_map/pallas_call | solution.py:571
  219.7 11.8 %shard_map.337 = (bf16[2048,384]{1,0:T(8,128)(2,1)}, bf16[1024,384]{1,0:T(8,128)(2,1)}, bf16[1024,384]{1,0:T(8,128)(2,1)}, f32[768,768]{1,0:T(8,128)S(1)}) custom-call(s32[5]{0:T(128)S(1)} %copy-done.5, bf16[4096,768]{1,0:T(8,128)(2,1)} %bitcast.56, bf16[2048,384]{1,0:T(8,128)(2,1)} %get-tuple-element.162.refs_2_, ...), custom_call_target="tpu_custom_call" | custom-call | flops 19327352832 | bytes 50331648 | tf_op jit(solution)/shard_map/pallas_call | solution.py:656
  232.0 12.3 %shard_map.338 = (bf16[1024,384]{1,0:T(8,128)(2,1)}, bf16[2048,384]{1,0:T(8,128)(2,1)}, bf16[2048,384]{1,0:T(8,128)(2,1)}) custom-call(s32[32]{0:T(128)S(1)} %get-tuple-element.138.scalars.refs_0_, bf16[1024,384]{1,0:T(8,128)(2,1)} %get-tuple-element.143.q.refs_1_, bf16[4096,768]{1,0:T(8,128)(2,1)} %shard_map.329.k.v.refs_2_.refs_3_, ...), custom_call_target="tpu_custom_call" | custom-call | flops 80530636800 | bytes 25165824 | tf_op jit(solution)/shard_map/pallas_call | solution.py:571
  245.9 9.5 %shard_map.339 = (bf16[2048,384]{1,0:T(8,128)(2,1)}, bf16[2048,384]{1,0:T(8,128)(2,1)}, bf16[2,192,1536]{2,1,0:T(8,128)(2,1)}, bf16[2,192,1536]{2,1,0:T(8,128)(2,1)}) custom-call(s32[5]{0:T(128)S(1)} %copy-done.5, bf16[4096,768]{1,0:T(8,128)(2,1)} %bitcast.57, bf16[2048,384]{1,0:T(8,128)(2,1)} %get-tuple-element.170.refs_2_, ...), custom_call_target="tpu_custom_call" | custom-call | flops 19327352832 | bytes 50331648 | tf_op jit(solution)/shard_map/pallas_call | solution.py:656
  255.5 6.0 %shard_map.340 = (bf16[2,192,1536]{2,1,0:T(8,128)(2,1)}, bf16[2,192,1536]{2,1,0:T(8,128)(2,1)}) custom-call(s32[5]{0:T(128)S(1)} %copy-done.5, bf16[1024,768]{1,0:T(8,128)(2,1)} %get-tuple-element.174.refs_0_, bf16[1024,768]{1,0:T(8,128)(2,1)} %get-tuple-element.148.refs_1_, ...), custom_call_target="tpu_custom_call", output_to_operand_aliasing={{0}: (7, {}), {1}: (8, {})} | custom-call | flops 4831838208 | bytes 25165824 | tf_op jit(solution)/shard_map/pallas_call | solution.py:785
  261.5 5.2 %collective-permute-start.20 = (bf16[2,192,1536]{2,1,0:T(8,128)(2,1)}, bf16[2,192,1536]{2,1,0:T(8,128)(2,1)}, u32[]{:S(2)}, u32[]{:S(2)}) collective-permute-start(bf16[2,192,1536]{2,1,0:T(8,128)(2,1)} %get-tuple-element.177), channel_id=1, source_target_pairs={{0,2},{2,0},{4,6},{6,4},{1,3},{3,1},{5,7},{7,5},{8,10},{10,8},{12,... | collective-permute-start | bytes 3538952 | tf_op jit(solution)/shard_map/ppermute | solution.py:1203
  276.2 9.8 %shard_map.341 = (bf16[1024,768]{1,0:T(8,128)(2,1)}, bf16[1024,384]{1,0:T(8,128)(2,1)S(1)}, f32[24,1024]{1,0:T(8,128)S(1)}, f32[8,768]{1,0:T(8,128)S(1)}) custom-call(s32[5]{0:T(128)S(1)} %copy-done.5, bf16[1024,768]{1,0:T(8,128)(2,1)} %get-tuple-element.148.refs_1_, bf16[1024,768]{1,0:T(8,128)(2,1)} %get-tuple-element.137.refs_1_.refs_2_, ...), custom_call_target="tpu_custom_call" | custom-call | flops 7247757312 | bytes 50331648 | tf_op jit(solution)/shard_map/pallas_call | solution.py:1049
  288.8 4.5 %shard_map.342 = (bf16[1024,128]{1,0:T(8,128)(2,1)}, bf16[1024,128]{1,0:T(8,128)(2,1)}, bf16[1024,128]{1,0:T(8,128)(2,1)}) custom-call(bf16[1024,1152]{1,0:T(8,128)(2,1)S(1)} %copy-done.21, bf16[1024,1152]{1,0:T(8,128)(2,1)S(1)} %copy-done.21, bf16[1024,1152]{1,0:T(8,128)(2,1)S(1)} %copy-done.21, bf16[1024,384]{1,0:T(8,128)(2,1)S(1)} %get-tuple-element.200.grad, ...), custom_call_target="tpu_custom_call" | custom-call | flops 13421772800 | bytes 8388608 | tf_op jit(solution)/shard_map/pallas_call | solution.py:404
  293.4 4.5 %shard_map.343 = (bf16[1024,128]{1,0:T(8,128)(2,1)}, bf16[1024,128]{1,0:T(8,128)(2,1)}, bf16[1024,128]{1,0:T(8,128)(2,1)}) custom-call(bf16[1024,1152]{1,0:T(8,128)(2,1)S(1)} %copy-done.21, bf16[1024,1152]{1,0:T(8,128)(2,1)S(1)} %copy-done.21, bf16[1024,1152]{1,0:T(8,128)(2,1)S(1)} %copy-done.21, bf16[1024,384]{1,0:T(8,128)(2,1)S(1)} %get-tuple-element.200.grad, ...), custom_call_target="tpu_custom_call" | custom-call | flops 13421772800 | bytes 8388608 | tf_op jit(solution)/shard_map/pallas_call | solution.py:404
  297.9 7.0 %shard_map.344 = (bf16[2,192,1152]{2,1,0:T(8,128)(2,1)}, bf16[2,192,1152]{2,1,0:T(8,128)(2,1)}) custom-call(s32[5]{0:T(128)S(1)} %copy-done.5, bf16[1024,768]{1,0:T(8,128)(2,1)} %get-tuple-element.188.refs_0_.refs_2_, bf16[1024,768]{1,0:T(8,128)(2,1)} %get-tuple-element.189.refs_1_.e1, bf16[1024,128]{1,0:T(8,128)(2,1)} %get-tuple-element.184.refs_2_.refs_5_, ...), custom_call_target="tpu_custom_call" | custom-call | flops 7247757312 | bytes 25165824 | tf_op jit(solution)/shard_map/pallas_call | solution.py:785
  306.4 8.2 %collective-permute-start.36 = (bf16[192,1536]{1,0:T(8,128)(2,1)S(1)}, bf16[192,1536]{1,0:T(8,128)(2,1)S(1)}, u32[]{:S(2)}, u32[]{:S(2)}) collective-permute-start(bf16[192,1536]{1,0:T(8,128)(2,1)S(1)} %fusion.4), channel_id=1, source_target_pairs={{0,8},{24,16},{1,9},{25,17},{2,10},{26,18},{3,11},{27,19},{4,12},{... | collective-permute-start | bytes 1769480 | tf_op jit(solution)/shard_map/ppermute | solution.py:1236
  314.6 4.6 %shard_map.345 = (bf16[1024,128]{1,0:T(8,128)(2,1)}, bf16[1024,128]{1,0:T(8,128)(2,1)}, bf16[1024,128]{1,0:T(8,128)(2,1)}) custom-call(bf16[1024,1152]{1,0:T(8,128)(2,1)S(1)} %copy-done.21, bf16[1024,1152]{1,0:T(8,128)(2,1)S(1)} %copy-done.21, bf16[1024,1152]{1,0:T(8,128)(2,1)S(1)} %copy-done.21, bf16[1024,384]{1,0:T(8,128)(2,1)S(1)} %get-tuple-element.200.grad, ...), custom_call_target="tpu_custom_call" | custom-call | flops 13421772800 | bytes 8388608 | tf_op jit(solution)/shard_map/pallas_call | solution.py:404
  321.4 7.7 %shard_map.346 = (bf16[1024,768]{1,0:T(8,128)(2,1)}, bf16[2,208,384]{2,1,0:T(8,128)(2,1)S(1)}, bf16[2,208,384]{2,1,0:T(8,128)(2,1)S(1)}) custom-call(s32[5]{0:T(128)S(1)} %copy-done.5, bf16[1024,768]{1,0:T(8,128)(2,1)} %get-tuple-element.196.x.refs_1_, bf16[1024,768]{1,0:T(8,128)(2,1)} %get-tuple-element.188.refs_0_.refs_2_, ...), custom_call_target="tpu_custom_call" | custom-call | flops 9663676416 | bytes 25165824 | tf_op jit(solution)/shard_map/pallas_call | solution.py:1132
  334.3 6.6 %collective-permute-start.32 = (bf16[192,1152]{1,0:T(8,128)(2,1)S(1)}, bf16[192,1152]{1,0:T(8,128)(2,1)S(1)}, u32[]{:S(2)}, u32[]{:S(2)}) collective-permute-start(bf16[192,1152]{1,0:T(8,128)(2,1)S(1)} %fusion.6), channel_id=1, source_target_pairs={{0,8},{24,16},{1,9},{25,17},{2,10},{26,18},{3,11},{27,19},{4,12},{... | collective-permute-start | bytes 1327112 | tf_op jit(solution)/shard_map/ppermute | solution.py:1236
  340.9 4.8 %shard_map.347 = bf16[1024,768]{1,0:T(8,128)(2,1)} custom-call(s32[8,1024]{1,0:T(8,128)S(1)} %copy-done.31, bf16[1024,768]{1,0:T(8,128)(2,1)} %get-tuple-element.206.values), custom_call_target="tpu_custom_call" | custom-call | flops 6442450944 | bytes 12582912 | tf_op jit(solution)/shard_map/pallas_call | solution.py:199
  358.9 9.9 %collective-permute-done.31 = bf16[208,384]{1,0:T(8,128)(2,1)S(1)} collective-permute-done((bf16[208,384]{1,0:T(8,128)(2,1)S(1)}, bf16[208,384]{1,0:T(8,128)(2,1)S(1)}, u32[]{:S(2)}, u32[]{:S(2)}) %collective-permute-start.31) | collective-permute-done | bytes 159776 | tf_op jit(solution)/shard_map/ppermute | solution.py:1249
  373.3 7.3 %shard_map.348 = bf16[1024,768]{1,0:T(8,128)(2,1)} custom-call(s32[8,1024]{1,0:T(8,128)S(1)} %copy-done.31, bf16[1024,768]{1,0:T(8,128)(2,1)} %get-tuple-element.189.refs_1_.e1, bf16[1024,768]{1,0:T(8,128)(2,1)} %get-tuple-element.196.x.refs_1_, bf16[1024,768]{1,0:T(8,128)(2,1)} %get-tuple-element.207.mine, ...), custom_call_target="tpu_custom_call" | custom-call | flops 6442450944 | bytes 37748736 | tf_op jit(solution)/shard_map/pallas_call | solution.py:1187
  381.8 5.5 %collective-permute-done.35 = bf16[192,1152]{1,0:T(8,128)(2,1)S(1)} collective-permute-done((bf16[192,1152]{1,0:T(8,128)(2,1)S(1)}, bf16[192,1152]{1,0:T(8,128)(2,1)S(1)}, u32[]{:S(2)}, u32[]{:S(2)}) %collective-permute-start.35) | collective-permute-done | bytes 442400 | tf_op jit(solution)/shard_map/ppermute | solution.py:1249
  (236 shorter events, 84.7 us)
Async XLA Ops:
  7.2 119.7 %all-gather.2.cloned.1.call-start = ((), (), s32[]{:S(2)}) async-start(), calls=%async_computation | async-start | bytes 13271040 | tf_op jit(solution)/shard_map/all_gather | solution.py:1211
  10.5 17.0 %collective-permute-start.2 = (bf16[208,1152]{1,0:T(8,128)(2,1)S(1)}, bf16[208,1152]{1,0:T(8,128)(2,1)S(1)}, u32[]{:S(2)}, u32[]{:S(2)}) collective-permute-start(bf16[208,1152]{1,0:T(8,128)(2,1)S(1)} %fusion.11.w0.refs_14_), channel_id=1, source_target_pairs={{0,4},{2,6},{4,0},{6,2},{1,5},{3,7},{5,1},{7,3},{8,12},{10,14},{12... | collective-permute-start | bytes 1437704 | tf_op jit(solution)/shard_map/ppermute | solution.py:1203
  13.5 7.4 %collective-permute-start = (bf16[208,1152]{1,0:T(8,128)(2,1)S(1)}, bf16[208,1152]{1,0:T(8,128)(2,1)S(1)}, u32[]{:S(2)}, u32[]{:S(2)}) collective-permute-start(bf16[208,1152]{1,0:T(8,128)(2,1)S(1)} %fusion.11.w0.refs_14_), channel_id=1, source_target_pairs={{0,2},{2,0},{4,6},{6,4},{1,3},{3,1},{5,7},{7,5},{8,10},{10,8},{12,... | collective-permute-start | bytes 1437704 | tf_op jit(solution)/shard_map/ppermute | solution.py:1203
  27.5 245.5 %all-reduce.3.cloned.1.call-start = ((), (), s32[]{:S(2)}) async-start(), calls=%async_computation.1 | async-start | bytes 2359296 | tf_op jit(solution)/shard_map/psum | solution.py:1406
  28.4 9.3 %collective-permute-start.4 = (bf16[192,1536]{1,0:T(8,128)(2,1)S(1)}, bf16[192,1536]{1,0:T(8,128)(2,1)S(1)}, u32[]{:S(2)}, u32[]{:S(2)}) collective-permute-start(bf16[192,1536]{1,0:T(8,128)(2,1)S(1)} %constant_dynamic-update-slice_fusion.refs_1_.refs_9_.refs_4_), channel_id=1, source_target_pairs={{0,2},{2,0},{4,6},{6,4},{1,3},{3,1},{5,7},{7,5},{8,10},{10,8},{12,... | collective-permute-start | bytes 1769480 | tf_op jit(solution)/shard_map/ppermute | solution.py:1203
  29.3 19.6 %collective-permute-start.6 = (bf16[192,384]{1,0:T(8,128)(2,1)S(1)}, bf16[192,384]{1,0:T(8,128)(2,1)S(1)}, u32[]{:S(2)}, u32[]{:S(2)}) collective-permute-start(bf16[192,384]{1,0:T(8,128)(2,1)S(1)} %collective-permute-done.1.refs_13_), channel_id=1, source_target_pairs={{0,2},{2,0},{4,6},{6,4},{1,3},{3,1},{5,7},{7,5},{8,10},{10,8},{12,... | collective-permute-start | bytes 442376 | tf_op jit(solution)/shard_map/ppermute | solution.py:1203
  29.5 13.1 %collective-permute-start.5 = (bf16[192,384]{1,0:T(8,128)(2,1)S(1)}, bf16[192,384]{1,0:T(8,128)(2,1)S(1)}, u32[]{:S(2)}, u32[]{:S(2)}) collective-permute-start(bf16[192,384]{1,0:T(8,128)(2,1)S(1)} %collective-permute-done.1.refs_13_), channel_id=1, source_target_pairs={{0,4},{2,6},{4,0},{6,2},{1,5},{3,7},{5,1},{7,3},{8,12},{10,14},{12... | collective-permute-start | bytes 442376 | tf_op jit(solution)/shard_map/ppermute | solution.py:1203
  30.0 28.8 %collective-permute-start.9 = (bf16[192,1536]{1,0:T(8,128)(2,1)S(1)}, bf16[192,1536]{1,0:T(8,128)(2,1)S(1)}, u32[]{:S(2)}, u32[]{:S(2)}) collective-permute-start(bf16[192,1536]{1,0:T(8,128)(2,1)S(1)} %constant_dynamic-update-slice_fusion.refs_1_.refs_9_.refs_4_), channel_id=1, source_target_pairs={{0,4},{2,6},{4,0},{6,2},{1,5},{3,7},{5,1},{7,3},{8,12},{10,14},{12... | collective-permute-start | bytes 1769480 | tf_op jit(solution)/shard_map/ppermute | solution.py:1203
  42.2 21.8 %collective-permute-start.8 = (bf16[1024,128]{1,0:T(8,128)(2,1)}, bf16[1024,128]{1,0:T(8,128)(2,1)S(1)}, u32[]{:S(2)}, u32[]{:S(2)}) collective-permute-start(bf16[1024,128]{1,0:T(8,128)(2,1)} %get-tuple-element.126.refs_3_.refs_6_.refs_8_), channel_id=1, source_target_pairs={{0,1},{1,0},{2,3},{3,2},{4,5},{5,4},{6,7},{7,6},{8,9},{9,8},{10,11... | collective-permute-start | bytes 786440 | tf_op jit(solution)/shard_map/ppermute | solution.py:1203
  47.2 26.4 %collective-permute-start.11 = (bf16[1024,128]{1,0:T(8,128)(2,1)}, bf16[1024,128]{1,0:T(8,128)(2,1)S(1)}, u32[]{:S(2)}, u32[]{:S(2)}) collective-permute-start(bf16[1024,128]{1,0:T(8,128)(2,1)} %get-tuple-element.128.refs_4_.refs_7_.refs_9_), channel_id=1, source_target_pairs={{0,1},{1,0},{2,3},{3,2},{4,5},{5,4},{6,7},{7,6},{8,9},{9,8},{10,11... | collective-permute-start | bytes 786440 | tf_op jit(solution)/shard_map/ppermute | solution.py:1203
  53.4 20.2 %collective-permute-start.12 = (bf16[1024,128]{1,0:T(8,128)(2,1)}, bf16[1024,128]{1,0:T(8,128)(2,1)S(1)}, u32[]{:S(2)}, u32[]{:S(2)}) collective-permute-start(bf16[1024,128]{1,0:T(8,128)(2,1)} %get-tuple-element.131.refs_5_.refs_8_.refs_10_), channel_id=1, source_target_pairs={{0,1},{1,0},{2,3},{3,2},{4,5},{5,4},{6,7},{7,6},{8,9},{9,8},{10,11... | collective-permute-start | bytes 786440 | tf_op jit(solution)/shard_map/ppermute | solution.py:1203
  92.7 14.9 %collective-permute-start.13 = (bf16[1024,128]{1,0:T(8,128)(2,1)}, bf16[1024,128]{1,0:T(8,128)(2,1)S(1)}, u32[]{:S(2)}, u32[]{:S(2)}) collective-permute-start(bf16[1024,128]{1,0:T(8,128)(2,1)} %get-tuple-element.140.refs_4_.refs_3_), channel_id=1, source_target_pairs={{0,1},{1,0},{2,3},{3,2},{4,5},{5,4},{6,7},{7,6},{8,9},{9,8},{10,11... | collective-permute-start | bytes 786440 | tf_op jit(solution)/shard_map/ppermute | solution.py:1203
  103.8 15.0 %collective-permute-start.14 = (bf16[1024,128]{1,0:T(8,128)(2,1)}, bf16[1024,128]{1,0:T(8,128)(2,1)}, u32[]{:S(2)}, u32[]{:S(2)}) collective-permute-start(bf16[1024,128]{1,0:T(8,128)(2,1)} %get-tuple-element.142.refs_5_.refs_4_), channel_id=1, source_target_pairs={{0,1},{1,0},{2,3},{3,2},{4,5},{5,4},{6,7},{7,6},{8,9},{9,8},{10,11... | collective-permute-start | bytes 786440 | tf_op jit(solution)/shard_map/ppermute | solution.py:1203
  118.8 8.1 %collective-permute-start.15 = (bf16[1024,128]{1,0:T(8,128)(2,1)}, bf16[1024,128]{1,0:T(8,128)(2,1)}, u32[]{:S(2)}, u32[]{:S(2)}) collective-permute-start(bf16[1024,128]{1,0:T(8,128)(2,1)} %get-tuple-element.144.refs_6_.refs_5_), channel_id=1, source_target_pairs={{0,1},{1,0},{2,3},{3,2},{4,5},{5,4},{6,7},{7,6},{8,9},{9,8},{10,11... | collective-permute-start | bytes 786440 | tf_op jit(solution)/shard_map/ppermute | solution.py:1203
  176.8 39.1 %collective-permute-start.17 = (bf16[192,3072]{1,0:T(8,128)(2,1)S(1)}, bf16[192,3072]{1,0:T(8,128)(2,1)S(1)}, u32[]{:S(2)}, u32[]{:S(2)}) collective-permute-start(bf16[192,3072]{1,0:T(8,128)(2,1)S(1)} %fusion.2), channel_id=1, source_target_pairs={{0,4},{2,6},{4,0},{6,2},{1,5},{3,7},{5,1},{7,3},{8,12},{10,14},{12... | collective-permute-start | bytes 3538952 | tf_op jit(solution)/shard_map/ppermute | solution.py:1203
  231.5 14.4 %collective-permute-start.18 = (bf16[1024,384]{1,0:T(8,128)(2,1)}, bf16[1024,384]{1,0:T(8,128)(2,1)S(1)}, u32[]{:S(2)}, u32[]{:S(2)}) collective-permute-start(bf16[1024,384]{1,0:T(8,128)(2,1)} %get-tuple-element.164), channel_id=1, source_target_pairs={{0,1},{1,0},{2,3},{3,2},{4,5},{5,4},{6,7},{7,6},{8,9},{9,8},{10,11... | collective-permute-start | bytes 2359304 | tf_op jit(solution)/shard_map/ppermute | solution.py:1203
  244.3 22.8 %collective-permute-start.19 = (bf16[1024,384]{1,0:T(8,128)(2,1)}, bf16[1024,384]{1,0:T(8,128)(2,1)S(1)}, u32[]{:S(2)}, u32[]{:S(2)}) collective-permute-start(bf16[1024,384]{1,0:T(8,128)(2,1)} %get-tuple-element.178.refs_2_.refs_3_), channel_id=1, source_target_pairs={{0,1},{1,0},{2,3},{3,2},{4,5},{5,4},{6,7},{7,6},{8,9},{9,8},{10,11... | collective-permute-start | bytes 2359304 | tf_op jit(solution)/shard_map/ppermute | solution.py:1203
  261.5 24.5 %collective-permute-start.20 = (bf16[2,192,1536]{2,1,0:T(8,128)(2,1)}, bf16[2,192,1536]{2,1,0:T(8,128)(2,1)}, u32[]{:S(2)}, u32[]{:S(2)}) collective-permute-start(bf16[2,192,1536]{2,1,0:T(8,128)(2,1)} %get-tuple-element.177), channel_id=1, source_target_pairs={{0,2},{2,0},{4,6},{6,4},{1,3},{3,1},{5,7},{7,5},{8,10},{10,8},{12,... | collective-permute-start | bytes 3538952 | tf_op jit(solution)/shard_map/ppermute | solution.py:1203
  266.8 62.7 %collective-permute-start.25 = (bf16[1024,384]{1,0:T(8,128)(2,1)}, bf16[1024,384]{1,0:T(8,128)(2,1)}, u32[]{:S(2)}, u32[]{:S(2)}) collective-permute-start(bf16[1024,384]{1,0:T(8,128)(2,1)} %get-tuple-element.211), channel_id=1, source_target_pairs={{0,1},{1,0},{2,3},{3,2},{4,5},{5,4},{6,7},{7,6},{8,9},{9,8},{10,11... | collective-permute-start | bytes 2359304 | tf_op jit(solution)/shard_map/ppermute | solution.py:1203
  267.1 64.1 %collective-permute-start.26 = (bf16[2048,384]{1,0:T(8,128)(2,1)}, bf16[2048,384]{1,0:T(8,128)(2,1)}, u32[]{:S(2)}, u32[]{:S(2)}) collective-permute-start(bf16[2048,384]{1,0:T(8,128)(2,1)} %get-tuple-element.215), channel_id=1, source_target_pairs={{0,1},{1,0},{2,3},{3,2},{4,5},{5,4},{6,7},{7,6},{8,9},{9,8},{10,11... | collective-permute-start | bytes 4718600 | tf_op jit(solution)/shard_map/ppermute | solution.py:1203
  287.3 17.8 %collective-permute-start.22 = (bf16[192,1536]{1,0:T(8,128)(2,1)S(1)}, bf16[192,1536]{1,0:T(8,128)(2,1)S(1)}, u32[]{:S(2)}, u32[]{:S(2)}) collective-permute-start(bf16[192,1536]{1,0:T(8,128)(2,1)S(1)} %fusion.9), channel_id=1, source_target_pairs={{0,4},{2,6},{4,0},{6,2},{1,5},{3,7},{5,1},{7,3},{8,12},{10,14},{12... | collective-permute-start | bytes 1769480 | tf_op jit(solution)/shard_map/ppermute | solution.py:1203
  305.0 14.2 %collective-permute-start.21 = (bf16[2,192,1152]{2,1,0:T(8,128)(2,1)}, bf16[2,192,1152]{2,1,0:T(8,128)(2,1)S(1)}, u32[]{:S(2)}, u32[]{:S(2)}) collective-permute-start(bf16[2,192,1152]{2,1,0:T(8,128)(2,1)} %get-tuple-element.195), channel_id=1, source_target_pairs={{0,2},{2,0},{4,6},{6,4},{1,3},{3,1},{5,7},{7,5},{8,10},{10,8},{12,... | collective-permute-start | bytes 2654216 | tf_op jit(solution)/shard_map/ppermute | solution.py:1203
  306.4 26.6 %collective-permute-start.36 = (bf16[192,1536]{1,0:T(8,128)(2,1)S(1)}, bf16[192,1536]{1,0:T(8,128)(2,1)S(1)}, u32[]{:S(2)}, u32[]{:S(2)}) collective-permute-start(bf16[192,1536]{1,0:T(8,128)(2,1)S(1)} %fusion.4), channel_id=1, source_target_pairs={{0,8},{24,16},{1,9},{25,17},{2,10},{26,18},{3,11},{27,19},{4,12},{... | collective-permute-start | bytes 1769480 | tf_op jit(solution)/shard_map/ppermute | solution.py:1236
  319.3 14.8 %collective-permute-start.23 = (bf16[192,1152]{1,0:T(8,128)(2,1)S(1)}, bf16[192,1152]{1,0:T(8,128)(2,1)S(1)}, u32[]{:S(2)}, u32[]{:S(2)}) collective-permute-start(bf16[192,1152]{1,0:T(8,128)(2,1)S(1)} %fusion.12), channel_id=1, source_target_pairs={{0,4},{2,6},{4,0},{6,2},{1,5},{3,7},{5,1},{7,3},{8,12},{10,14},{12... | collective-permute-start | bytes 1327112 | tf_op jit(solution)/shard_map/ppermute | solution.py:1203
  329.0 44.3 %collective-permute-start.24 = (bf16[1024,768]{1,0:T(8,128)(2,1)}, bf16[1024,768]{1,0:T(8,128)(2,1)S(1)}, u32[]{:S(2)}, u32[]{:S(2)}) collective-permute-start(bf16[1024,768]{1,0:T(8,128)(2,1)} %get-tuple-element.207.mine), channel_id=1, source_target_pairs={{0,1},{1,0},{2,3},{3,2},{4,5},{5,4},{6,7},{7,6},{8,9},{9,8},{10,11... | collective-permute-start | bytes 4718600 | tf_op jit(solution)/shard_map/ppermute | solution.py:1203
  333.2 23.4 %collective-permute-start.37 = (bf16[192,1536]{1,0:T(8,128)(2,1)S(1)}, bf16[192,1536]{1,0:T(8,128)(2,1)S(1)}, u32[]{:S(2)}, u32[]{:S(2)}) collective-permute-start(bf16[192,1536]{1,0:T(8,128)(2,1)S(1)} %fusion.7), channel_id=1, source_target_pairs={{8,16},{16,8},{9,17},{17,9},{10,18},{18,10},{11,19},{19,11},{12,20... | collective-permute-start | bytes 1769480 | tf_op jit(solution)/shard_map/ppermute | solution.py:1243
  334.0 11.8 %collective-permute-start.28 = (bf16[208,384]{1,0:T(8,128)(2,1)S(1)}, bf16[208,384]{1,0:T(8,128)(2,1)S(1)}, u32[]{:S(2)}, u32[]{:S(2)}) collective-permute-start(bf16[208,384]{1,0:T(8,128)(2,1)S(1)} %fusion.17), channel_id=1, source_target_pairs={{0,4},{2,6},{4,0},{6,2},{1,5},{3,7},{5,1},{7,3},{8,12},{10,14},{12... | collective-permute-start | bytes 479240 | tf_op jit(solution)/shard_map/ppermute | solution.py:1203
  334.3 23.8 %collective-permute-start.32 = (bf16[192,1152]{1,0:T(8,128)(2,1)S(1)}, bf16[192,1152]{1,0:T(8,128)(2,1)S(1)}, u32[]{:S(2)}, u32[]{:S(2)}) collective-permute-start(bf16[192,1152]{1,0:T(8,128)(2,1)S(1)} %fusion.6), channel_id=1, source_target_pairs={{0,8},{24,16},{1,9},{25,17},{2,10},{26,18},{3,11},{27,19},{4,12},{... | collective-permute-start | bytes 1327112 | tf_op jit(solution)/shard_map/ppermute | solution.py:1236
  355.3 13.5 %collective-permute-start.31 = (bf16[208,384]{1,0:T(8,128)(2,1)S(1)}, bf16[208,384]{1,0:T(8,128)(2,1)S(1)}, u32[]{:S(2)}, u32[]{:S(2)}) collective-permute-start(bf16[208,384]{1,0:T(8,128)(2,1)S(1)} %add_convert_fusion.12), channel_id=1, source_target_pairs={{8,0},{16,24},{9,1},{17,25},{10,2},{18,26},{11,3},{19,27},{12,4},{... | collective-permute-start | bytes 479240 | tf_op jit(solution)/shard_map/ppermute | solution.py:1249
  356.7 23.9 %collective-permute-start.38 = (bf16[192,1536]{1,0:T(8,128)(2,1)S(1)}, bf16[192,1536]{1,0:T(8,128)(2,1)S(1)}, u32[]{:S(2)}, u32[]{:S(2)}) collective-permute-start(bf16[192,1536]{1,0:T(8,128)(2,1)S(1)} %add_convert_fusion.4), channel_id=1, source_target_pairs={{8,0},{16,24},{9,1},{17,25},{10,2},{18,26},{11,3},{19,27},{12,4},{... | collective-permute-start | bytes 1769480 | tf_op jit(solution)/shard_map/ppermute | solution.py:1249
  358.2 10.6 %collective-permute-start.33 = (bf16[192,1152]{1,0:T(8,128)(2,1)S(1)}, bf16[192,1152]{1,0:T(8,128)(2,1)S(1)}, u32[]{:S(2)}, u32[]{:S(2)}) collective-permute-start(bf16[192,1152]{1,0:T(8,128)(2,1)S(1)} %fusion.8), channel_id=1, source_target_pairs={{8,16},{16,8},{9,17},{17,9},{10,18},{18,10},{11,19},{19,11},{12,20... | collective-permute-start | bytes 1327112 | tf_op jit(solution)/shard_map/ppermute | solution.py:1243
  369.4 17.9 %collective-permute-start.35 = (bf16[192,1152]{1,0:T(8,128)(2,1)S(1)}, bf16[192,1152]{1,0:T(8,128)(2,1)S(1)}, u32[]{:S(2)}, u32[]{:S(2)}) collective-permute-start(bf16[192,1152]{1,0:T(8,128)(2,1)S(1)} %add_convert_fusion.8), channel_id=1, source_target_pairs={{8,0},{16,24},{9,1},{17,25},{10,2},{18,26},{11,3},{19,27},{12,4},{... | collective-permute-start | bytes 1327112 | tf_op jit(solution)/shard_map/ppermute | solution.py:1249
  (61 other events, 770.7 us)
Sparse Core Ops, SparseCore 0:
  27.6 86.2 all-gather.1
  217.7 55.2 all-reduce.2
where the time goes:
time: 398 us; the launch traced here: 397 us
  Pallas kernels  253 us (64%)
  starting transfers between devices  48.9 us (12%)
  waiting for transfers between devices  45 us (11%)
  other arithmetic  19.9 us (5%)
  local copies, waits for them, and re-layouts  15.2 us (4%)
  between operations  15.2 us (4%)
    pallas_call x2, Pallas kernels, cross_backward(): pl.pallas_call(second_kernel if image else first_kernel, grid_spec=pltpu....  50.8 us
    pallas_call x3, Pallas kernels, cross_forward(): pl.pallas_call(cross_forward_kernel, grid_spec=pltpu.PrefetchScalarGridSp...  33.3 us
    pallas_call x1, Pallas kernels, units_step(): pl.pallas_call(kernel, grid=(count // ROWS,), in_specs=[SCALARS, rows(wid...  33 us
    ppermute x30, starting transfers between devices, swap(): return lax.ppermute(values, axis, [(i, i ^ distance) for i in range(size)])  26.5 us
    pallas_call x3, Pallas kernels, weight_grads(): pl.pallas_call(kernel, grid=(len(plan),), in_specs=[SCALARS] + [ANY] * (l...  23.4 us
    ppermute x30, waiting for transfers between devices, swap(): return lax.ppermute(values, axis, [(i, i ^ distance) for i in range(size)])  21.7 us
    pallas_call x2, Pallas kernels, memory_back(): pl.pallas_call(kernel, grid=(steps,), in_specs=[SCALARS, pl.BlockSpec((BA...  21.3 us
    ppermute x3, starting transfers between devices, line_first(): got = lax.ppermute(values, 'dp', [(0, 1), (3, 2)])  16.1 us
  transfers between devices with their start and end apart: 41, of which 9 were waited for; matrix products, arithmetic and copies ran while one was open for 5% of the time, Pallas kernels for 53%

commit v1 on v0

--- a/solution.py
+++ b/solution.py
@@ -623,13 +623,9 @@
         send_part[...] = leave
     else:
 
-        @pl.when(pl.program_id(0) < pl.num_programs(0) // 2)
-        def _():
-            send_part[...] = leave
-
-        @pl.when(pl.program_id(0) >= pl.num_programs(0) // 2)
-        def _():
-            send_more[...] = leave
+        early = pl.program_id(0) < pl.num_programs(0) // 2
+        send_part[...] = jnp.where(early, leave, send_part[...])
+        send_more[...] = leave
 
     keep_part[...] = jnp.where(side == 0, lower, upper)
     total[...] += dot(memory[...], both, TN)
@@ -1492,9 +1488,12 @@
     tokens_grad = last_step(pos, e1, x, dn1, dn1_theirs, all_gains[0])
     memory_grad = jnp.stack([after(memory0, self_part), memory1])
     cross_sum = line_third(line_second(cross_part), tokens_grad)
-    self_second = line_second(line_first(self_part))
+    self_first = line_first(self_part)
+    self_second = line_second(self_first)
     self_sum = line_third(self_second, tokens_grad)
-    last_sum = line_third(line_second(line_first(last_part)))
+    last_first = after(line_first(last_part), self_first)
+    last_second = after(line_second(last_first), self_second)
+    last_sum = line_third(last_second)
     gain_sums = last_sum[share:, :share].astype(F32)
     first_gain = gain_sums[0] + swap(after(gain_sums, self_second), "narrow", 1)[0]
 

time: 398 us -> 404 us (1.015); the launches traced: 397 us -> 398 us
  waiting for transfers between devices: 45 us -> 59 us
  starting transfers between devices: 48.9 us -> 39.3 us
    ppermute x30, waiting for transfers between devices: 21.7 us -> 30.6 us  [swap(): return lax.ppermute(values, axis, [(i, i ^ distance) for i in range(size)])]
    ppermute x3, waiting for transfers between devices: 15.4 us -> 24.1 us  [line_third(): got = after(lax.ppermute(values, 'dp', [(1, 0), (2, 3)]), *others)]
    ppermute x30, starting transfers between devices: 26.5 us -> 21.5 us  [swap(): return lax.ppermute(values, axis, [(i, i ^ distance) for i in range(size)])]
    ppermute x3, starting transfers between devices: 16.1 us -> 11.5 us  [line_first(): got = lax.ppermute(values, 'dp', [(0, 1), (3, 2)])]
    psum x1, waiting for transfers between devices: 4.21 us -> 0.01 us  [local(): unit_sum = lax.psum(unit_part, 'dp')]
  transfers between devices with their start and end apart: 41 -> 41, of which waited for: 9 -> 11; matrix products, arithmetic and copies ran while one was open for 5% -> 5% of each run, Pallas kernels for 53% -> 52%
where the time goes in v1:
time: 404 us; the launch traced here: 398 us
  Pallas kernels  250 us (62%)
  waiting for transfers between devices  59 us (15%)
  starting transfers between devices  39.3 us (10%)
  other arithmetic  19.9 us (5%)
  local copies, waits for them, and re-layouts  15.2 us (4%)
  between operations  15.2 us (4%)
    pallas_call x2, Pallas kernels, cross_backward(): pl.pallas_call(second_kernel if image else first_kernel, grid_spec=pltpu....  50.8 us
    pallas_call x3, Pallas kernels, cross_forward(): pl.pallas_call(cross_forward_kernel, grid_spec=pltpu.PrefetchScalarGridSp...  33.4 us
    pallas_call x1, Pallas kernels, units_step(): pl.pallas_call(kernel, grid=(count // ROWS,), in_specs=[SCALARS, rows(wid...  33.3 us
    ppermute x30, waiting for transfers between devices, swap(): return lax.ppermute(values, axis, [(i, i ^ distance) for i in range(size)])  30.6 us
    ppermute x3, waiting for transfers between devices, line_third(): got = after(lax.ppermute(values, 'dp', [(1, 0), (2, 3)]), *others)  24.1 us
    pallas_call x3, Pallas kernels, weight_grads(): pl.pallas_call(kernel, grid=(len(plan),), in_specs=[SCALARS] + [ANY] * (l...  23.3 us
    ppermute x30, starting transfers between devices, swap(): return lax.ppermute(values, axis, [(i, i ^ distance) for i in range(size)])  21.5 us
    pallas_call x2, Pallas kernels, memory_back(): pl.pallas_call(kernel, grid=(steps,), in_specs=[SCALARS, pl.BlockSpec((BA...  18.6 us
  transfers between devices with their start and end apart: 41, of which 11 were waited for; matrix products, arithmetic and copies ran while one was open for 5% of the time, Pallas kernels for 52%

profile of v1, /device:TPU:0, one launch (start us, length us, event | category | flops | bytes accessed | tf_op | source)
XLA Modules:
  0.0 398.2 jit_solution(2796525049025168046)
XLA Ops:
  20.9 5.8 %shard_map.323 = (bf16[1024,768]{1,0:T(8,128)(2,1)}, f32[8,1024]{1,0:T(8,128)S(1)}, f32[1024,128]{1,0:T(8,128)S(1)}, s32[8,1024]{1,0:T(8,128)S(1)}, s32[32]{0:T(128)S(1)}) custom-call(s32[1,1024]{1,0:T(1,128)S(1)} %copy-done.17, s32[1,1024]{1,0:T(1,128)S(1)} %copy-done.18, s32[1,8]{1,0:T(1,128)S(1)} %copy-done.19, bf16[1024,768]{1,0:T(8,128)(2,1)} %x.2), custom_call_target="tpu_custom_call" | custom-call | flops 6442450944 | bytes 25165824 | tf_op jit(solution)/shard_map/pallas_call | solution.py:140
  32.3 5.3 %shard_map.324 = (bf16[1024,768]{1,0:T(8,128)(2,1)}, bf16[1024,1152]{1,0:T(8,128)(2,1)S(1)}) custom-call(s32[5]{0:T(128)S(1)} %stack.65.places.refs_0_, bf16[1024,768]{1,0:T(8,128)(2,1)} %get-tuple-element.198.x.refs_1_, f32[1,768]{1,0:T(1,128)S(1)} %get-tuple-element.251.gain, bf16[208,1152]{1,0:T(8,128)(2,1)S(1)} %fusion.11.w0.refs_14_, ...), custom_call_target="tpu_custom_call" | custom-call | flops 7247757312 | bytes 22020096 | tf_op jit(solution)/shard_map/pallas_call | solution.py:259
  37.7 4.5 %shard_map.325 = (bf16[1024,128]{1,0:T(8,128)(2,1)}, f32[8,1024]{1,0:T(8,128)}) custom-call(bf16[1024,1152]{1,0:T(8,128)(2,1)S(1)} %get-tuple-element.132.q.k.v, bf16[1024,1152]{1,0:T(8,128)(2,1)S(1)} %get-tuple-element.132.q.k.v, bf16[1024,1152]{1,0:T(8,128)(2,1)S(1)} %get-tuple-element.132.q.k.v, f32[8,1024]{1,0:T(8,128)S(1)} %get-tuple-element.126.row_ids, ...), custom_call_target="tpu_custom_call" | custom-call | flops 5368709120 | bytes 4194304 | tf_op jit(solution)/shard_map/pallas_call | solution.py:351
  42.6 4.5 %shard_map.326 = (bf16[1024,128]{1,0:T(8,128)(2,1)}, f32[8,1024]{1,0:T(8,128)}) custom-call(bf16[1024,1152]{1,0:T(8,128)(2,1)S(1)} %get-tuple-element.132.q.k.v, bf16[1024,1152]{1,0:T(8,128)(2,1)S(1)} %get-tuple-element.132.q.k.v, bf16[1024,1152]{1,0:T(8,128)(2,1)S(1)} %get-tuple-element.132.q.k.v, f32[8,1024]{1,0:T(8,128)S(1)} %get-tuple-element.126.row_ids, ...), custom_call_target="tpu_custom_call" | custom-call | flops 5368709120 | bytes 4194304 | tf_op jit(solution)/shard_map/pallas_call | solution.py:351
  53.7 5.1 %collective-permute-done.9.refs_2_.refs_10_.refs_5_ = bf16[192,1536]{1,0:T(8,128)(2,1)S(1)} collective-permute-done((bf16[192,1536]{1,0:T(8,128)(2,1)S(1)}, bf16[192,1536]{1,0:T(8,128)(2,1)S(1)}, u32[]{:S(2)}, u32[]{:S(2)}) %collective-permute-start.9) | collective-permute-done | bytes 589856 | tf_op jit(solution)/shard_map/ppermute | solution.py:1199
  58.8 5.0 %shard_map.328.refs_3_.refs_1_ = bf16[1024,768]{1,0:T(8,128)(2,1)} custom-call(s32[8,1024]{1,0:T(8,128)S(1)} %get-tuple-element.122.pos, bf16[1024,768]{1,0:T(8,128)(2,1)} %values), custom_call_target="tpu_custom_call" | custom-call | flops 6442450944 | bytes 12582912 | tf_op jit(solution)/shard_map/pallas_call | solution.py:178
  63.8 9.3 %shard_map.329.k.v.refs_2_.refs_3_ = bf16[4096,768]{1,0:T(8,128)(2,1)} custom-call(s32[5]{0:T(128)S(1)} %stack.65.places.refs_0_, bf16[4096,768]{1,0:T(8,128)(2,1)} %bitcast.55, bf16[192,1536]{1,0:T(8,128)(2,1)S(1)} %constant_dynamic-update-slice_fusion.refs_1_.refs_9_.refs_4_, bf16[192,1536]{1,0:T(8,128)(2,1)S(1)} %collective-permute-done.9.refs_2_.refs_10_.refs_5_, ...), custom_call_target="tpu_custom_call" | custom-call | flops 19327352832 | bytes 50331648 | tf_op jit(solution)/shard_map/pallas_call | solution.py:292
  73.2 7.9 %shard_map.330 = (bf16[1024,768]{1,0:T(8,128)(2,1)}, bf16[1024,768]{1,0:T(8,128)(2,1)}, bf16[1024,384]{1,0:T(8,128)(2,1)}) custom-call(s32[5]{0:T(128)S(1)} %stack.65.places.refs_0_, bf16[1024,768]{1,0:T(8,128)(2,1)} %get-tuple-element.198.x.refs_1_, f32[1,768]{1,0:T(1,128)S(1)} %get-tuple-element.250.refs_2_.refs_5_, ...), custom_call_target="tpu_custom_call" | custom-call | flops 7247757312 | bytes 37748736 | tf_op jit(solution)/shard_map/pallas_call | solution.py:839
  81.1 11.1 %shard_map.331 = (bf16[1024,128]{1,0:T(8,128)(2,1)}, f32[8,1024]{1,0:T(8,128)}) custom-call(s32[32]{0:T(128)S(1)} %get-tuple-element.140.scalars.refs_0_, bf16[1024,384]{1,0:T(8,128)(2,1)} %get-tuple-element.145.q.refs_1_, bf16[4096,768]{1,0:T(8,128)(2,1)} %shard_map.329.k.v.refs_2_.refs_3_, bf16[4096,768]{1,0:T(8,128)(2,1)} %shard_map.329.k.v.refs_2_.refs_3_), custom_call_target="tpu_custom_call" | custom-call | flops 21474836480 | bytes 8388608 | tf_op jit(solution)/shard_map/pallas_call | solution.py:483
  92.3 11.1 %shard_map.332 = (bf16[1024,128]{1,0:T(8,128)(2,1)}, f32[8,1024]{1,0:T(8,128)}) custom-call(s32[32]{0:T(128)S(1)} %get-tuple-element.140.scalars.refs_0_, bf16[1024,384]{1,0:T(8,128)(2,1)} %get-tuple-element.145.q.refs_1_, bf16[4096,768]{1,0:T(8,128)(2,1)} %shard_map.329.k.v.refs_2_.refs_3_, bf16[4096,768]{1,0:T(8,128)(2,1)} %shard_map.329.k.v.refs_2_.refs_3_), custom_call_target="tpu_custom_call" | custom-call | flops 21474836480 | bytes 8388608 | tf_op jit(solution)/shard_map/pallas_call | solution.py:483
  107.2 11.1 %shard_map.333 = (bf16[1024,128]{1,0:T(8,128)(2,1)}, f32[8,1024]{1,0:T(8,128)}) custom-call(s32[32]{0:T(128)S(1)} %get-tuple-element.140.scalars.refs_0_, bf16[1024,384]{1,0:T(8,128)(2,1)} %get-tuple-element.145.q.refs_1_, bf16[4096,768]{1,0:T(8,128)(2,1)} %shard_map.329.k.v.refs_2_.refs_3_, bf16[4096,768]{1,0:T(8,128)(2,1)} %shard_map.329.k.v.refs_2_.refs_3_), custom_call_target="tpu_custom_call" | custom-call | flops 21474836480 | bytes 8388608 | tf_op jit(solution)/shard_map/pallas_call | solution.py:483
  118.4 8.3 %collective-permute-done.15.refs_9_ = bf16[1024,128]{1,0:T(8,128)(2,1)} collective-permute-done((bf16[1024,128]{1,0:T(8,128)(2,1)}, bf16[1024,128]{1,0:T(8,128)(2,1)}, u32[]{:S(2)}, u32[]{:S(2)}) %collective-permute-start.15) | collective-permute-done | bytes 262176 | tf_op jit(solution)/shard_map/ppermute | solution.py:1199
  126.7 33.3 %shard_map.334 = (bf16[1024,768]{1,0:T(8,128)(2,1)}, bf16[1024,768]{1,0:T(8,128)(2,1)}, bf16[1024,1024]{1,0:T(8,128)(2,1)}, bf16[1024,1024]{1,0:T(8,128)(2,1)}, ...) custom-call(s32[5]{0:T(128)} %copy-done.4, ...), custom_call_target="tpu_custom_call" | custom-call | flops 96636764160 | bytes 94371840 | tf_op jit(solution)/shard_map/pallas_call | solution.py:970
  160.0 10.3 %shard_map.335 = (bf16[2,192,3072]{2,1,0:T(8,128)(2,1)}, bf16[2,192,3072]{2,1,0:T(8,128)(2,1)}) custom-call(s32[5]{0:T(128)S(1)} %copy-done.5, bf16[1024,768]{1,0:T(8,128)(2,1)} %get-tuple-element.152.refs_0_, bf16[1024,768]{1,0:T(8,128)(2,1)} %shard_map.328.refs_3_.refs_1_, bf16[1024,1024]{1,0:T(8,128)(2,1)} %get-tuple-element.153.refs_2_, ...), custom_call_target="tpu_custom_call" | custom-call | flops 19327352832 | bytes 37748736 | tf_op jit(solution)/shard_map/pallas_call | solution.py:781
  170.5 4.7 %collective-permute-done.16 = bf16[2,192,3072]{2,1,0:T(8,128)(2,1)S(1)} collective-permute-done((bf16[2,192,3072]{2,1,0:T(8,128)(2,1)}, bf16[2,192,3072]{2,1,0:T(8,128)(2,1)S(1)}, u32[]{:S(2)}, u32[]{:S(2)}) %collective-permute-start.16) | collective-permute-done | bytes 2359328 | tf_op jit(solution)/shard_map/ppermute | solution.py:1199
  177.4 21.1 %shard_map.336 = (bf16[1024,384]{1,0:T(8,128)(2,1)}, bf16[2048,384]{1,0:T(8,128)(2,1)}, bf16[2048,384]{1,0:T(8,128)(2,1)}) custom-call(s32[32]{0:T(128)S(1)} %get-tuple-element.140.scalars.refs_0_, bf16[1024,384]{1,0:T(8,128)(2,1)} %get-tuple-element.145.q.refs_1_, bf16[4096,768]{1,0:T(8,128)(2,1)} %shard_map.329.k.v.refs_2_.refs_3_, ...), custom_call_target="tpu_custom_call" | custom-call | flops 80530636800 | bytes 25165824 | tf_op jit(solution)/shard_map/pallas_call | solution.py:571
  198.4 6.5 %collective-permute-done.17 = bf16[192,3072]{1,0:T(8,128)(2,1)S(1)} collective-permute-done((bf16[192,3072]{1,0:T(8,128)(2,1)S(1)}, bf16[192,3072]{1,0:T(8,128)(2,1)S(1)}, u32[]{:S(2)}, u32[]{:S(2)}) %collective-permute-start.17) | collective-permute-done | bytes 1179680 | tf_op jit(solution)/shard_map/ppermute | solution.py:1199
  208.7 9.1 %shard_map.337 = (bf16[2048,384]{1,0:T(8,128)(2,1)}, bf16[1024,384]{1,0:T(8,128)(2,1)}, bf16[1024,384]{1,0:T(8,128)(2,1)}, f32[768,768]{1,0:T(8,128)S(1)}) custom-call(s32[5]{0:T(128)S(1)} %copy-done.5, bf16[4096,768]{1,0:T(8,128)(2,1)} %bitcast.56, bf16[2048,384]{1,0:T(8,128)(2,1)} %get-tuple-element.164.refs_2_, ...), custom_call_target="tpu_custom_call" | custom-call | flops 19327352832 | bytes 50331648 | tf_op jit(solution)/shard_map/pallas_call | solution.py:652
  218.3 29.8 %shard_map.338 = (bf16[1024,384]{1,0:T(8,128)(2,1)}, bf16[2048,384]{1,0:T(8,128)(2,1)}, bf16[2048,384]{1,0:T(8,128)(2,1)}) custom-call(s32[32]{0:T(128)S(1)} %get-tuple-element.140.scalars.refs_0_, bf16[1024,384]{1,0:T(8,128)(2,1)} %get-tuple-element.145.q.refs_1_, bf16[4096,768]{1,0:T(8,128)(2,1)} %shard_map.329.k.v.refs_2_.refs_3_, ...), custom_call_target="tpu_custom_call" | custom-call | flops 80530636800 | bytes 25165824 | tf_op jit(solution)/shard_map/pallas_call | solution.py:571
  249.7 9.4 %shard_map.339 = (bf16[2048,384]{1,0:T(8,128)(2,1)}, bf16[2048,384]{1,0:T(8,128)(2,1)}, bf16[2,192,1536]{2,1,0:T(8,128)(2,1)}, bf16[2,192,1536]{2,1,0:T(8,128)(2,1)}) custom-call(s32[5]{0:T(128)S(1)} %copy-done.5, bf16[4096,768]{1,0:T(8,128)(2,1)} %bitcast.57, bf16[2048,384]{1,0:T(8,128)(2,1)} %get-tuple-element.172.refs_2_, ...), custom_call_target="tpu_custom_call" | custom-call | flops 19327352832 | bytes 50331648 | tf_op jit(solution)/shard_map/pallas_call | solution.py:652
  259.2 6.0 %shard_map.340 = (bf16[2,192,1536]{2,1,0:T(8,128)(2,1)}, bf16[2,192,1536]{2,1,0:T(8,128)(2,1)}) custom-call(s32[5]{0:T(128)S(1)} %copy-done.5, bf16[1024,768]{1,0:T(8,128)(2,1)} %get-tuple-element.176.refs_0_, bf16[1024,768]{1,0:T(8,128)(2,1)} %get-tuple-element.150.refs_1_, ...), custom_call_target="tpu_custom_call", output_to_operand_aliasing={{0}: (7, {}), {1}: (8, {})} | custom-call | flops 4831838208 | bytes 25165824 | tf_op jit(solution)/shard_map/pallas_call | solution.py:781
  270.6 9.8 %shard_map.341 = (bf16[1024,768]{1,0:T(8,128)(2,1)}, bf16[1024,384]{1,0:T(8,128)(2,1)S(1)}, f32[24,1024]{1,0:T(8,128)S(1)}, f32[8,768]{1,0:T(8,128)S(1)}) custom-call(s32[5]{0:T(128)S(1)} %copy-done.5, bf16[1024,768]{1,0:T(8,128)(2,1)} %get-tuple-element.150.refs_1_, bf16[1024,768]{1,0:T(8,128)(2,1)} %get-tuple-element.139.refs_1_.refs_2_, ...), custom_call_target="tpu_custom_call" | custom-call | flops 7247757312 | bytes 50331648 | tf_op jit(solution)/shard_map/pallas_call | solution.py:1045
  282.2 4.5 %shard_map.342 = (bf16[1024,128]{1,0:T(8,128)(2,1)}, bf16[1024,128]{1,0:T(8,128)(2,1)}, bf16[1024,128]{1,0:T(8,128)(2,1)}) custom-call(bf16[1024,1152]{1,0:T(8,128)(2,1)S(1)} %copy-done.21, bf16[1024,1152]{1,0:T(8,128)(2,1)S(1)} %copy-done.21, bf16[1024,1152]{1,0:T(8,128)(2,1)S(1)} %copy-done.21, bf16[1024,384]{1,0:T(8,128)(2,1)S(1)} %get-tuple-element.202.grad, ...), custom_call_target="tpu_custom_call" | custom-call | flops 13421772800 | bytes 8388608 | tf_op jit(solution)/shard_map/pallas_call | solution.py:404
  286.8 4.5 %shard_map.343 = (bf16[1024,128]{1,0:T(8,128)(2,1)}, bf16[1024,128]{1,0:T(8,128)(2,1)}, bf16[1024,128]{1,0:T(8,128)(2,1)}) custom-call(bf16[1024,1152]{1,0:T(8,128)(2,1)S(1)} %copy-done.21, bf16[1024,1152]{1,0:T(8,128)(2,1)S(1)} %copy-done.21, bf16[1024,1152]{1,0:T(8,128)(2,1)S(1)} %copy-done.21, bf16[1024,384]{1,0:T(8,128)(2,1)S(1)} %get-tuple-element.202.grad, ...), custom_call_target="tpu_custom_call" | custom-call | flops 13421772800 | bytes 8388608 | tf_op jit(solution)/shard_map/pallas_call | solution.py:404
  291.3 7.0 %shard_map.344 = (bf16[2,192,1152]{2,1,0:T(8,128)(2,1)}, bf16[2,192,1152]{2,1,0:T(8,128)(2,1)}) custom-call(s32[5]{0:T(128)S(1)} %copy-done.5, bf16[1024,768]{1,0:T(8,128)(2,1)} %get-tuple-element.190.refs_0_.refs_2_, bf16[1024,768]{1,0:T(8,128)(2,1)} %get-tuple-element.191.refs_1_.e1, bf16[1024,128]{1,0:T(8,128)(2,1)} %get-tuple-element.186.refs_2_.refs_5_, ...), custom_call_target="tpu_custom_call" | custom-call | flops 7247757312 | bytes 25165824 | tf_op jit(solution)/shard_map/pallas_call | solution.py:781
  301.6 4.6 %shard_map.345 = (bf16[1024,128]{1,0:T(8,128)(2,1)}, bf16[1024,128]{1,0:T(8,128)(2,1)}, bf16[1024,128]{1,0:T(8,128)(2,1)}) custom-call(bf16[1024,1152]{1,0:T(8,128)(2,1)S(1)} %copy-done.21, bf16[1024,1152]{1,0:T(8,128)(2,1)S(1)} %copy-done.21, bf16[1024,1152]{1,0:T(8,128)(2,1)S(1)} %copy-done.21, bf16[1024,384]{1,0:T(8,128)(2,1)S(1)} %get-tuple-element.202.grad, ...), custom_call_target="tpu_custom_call" | custom-call | flops 13421772800 | bytes 8388608 | tf_op jit(solution)/shard_map/pallas_call | solution.py:404
  308.3 7.7 %shard_map.346 = (bf16[1024,768]{1,0:T(8,128)(2,1)}, bf16[2,208,384]{2,1,0:T(8,128)(2,1)S(1)}, bf16[2,208,384]{2,1,0:T(8,128)(2,1)S(1)}) custom-call(s32[5]{0:T(128)S(1)} %copy-done.5, bf16[1024,768]{1,0:T(8,128)(2,1)} %get-tuple-element.198.x.refs_1_, bf16[1024,768]{1,0:T(8,128)(2,1)} %get-tuple-element.190.refs_0_.refs_2_, ...), custom_call_target="tpu_custom_call" | custom-call | flops 9663676416 | bytes 25165824 | tf_op jit(solution)/shard_map/pallas_call | solution.py:1128
  323.2 8.4 %collective-permute-start.30 = (bf16[192,1152]{1,0:T(8,128)(2,1)S(1)}, bf16[192,1152]{1,0:T(8,128)(2,1)S(1)}, u32[]{:S(2)}, u32[]{:S(2)}) collective-permute-start(bf16[192,1152]{1,0:T(8,128)(2,1)S(1)} %fusion.6), channel_id=1, source_target_pairs={{0,8},{24,16},{1,9},{25,17},{2,10},{26,18},{3,11},{27,19},{4,12},{... | collective-permute-start | bytes 1327112 | tf_op jit(solution)/shard_map/ppermute | solution.py:1232
  331.7 4.8 %shard_map.347 = bf16[1024,768]{1,0:T(8,128)(2,1)} custom-call(s32[8,1024]{1,0:T(8,128)S(1)} %copy-done.31, bf16[1024,768]{1,0:T(8,128)(2,1)} %get-tuple-element.208.values), custom_call_target="tpu_custom_call" | custom-call | flops 6442450944 | bytes 12582912 | tf_op jit(solution)/shard_map/pallas_call | solution.py:199
  351.8 17.8 %collective-permute-done.33 = bf16[208,384]{1,0:T(8,128)(2,1)S(1)} collective-permute-done((bf16[208,384]{1,0:T(8,128)(2,1)S(1)}, bf16[208,384]{1,0:T(8,128)(2,1)S(1)}, u32[]{:S(2)}, u32[]{:S(2)}) %collective-permute-start.33) | collective-permute-done | bytes 159776 | tf_op jit(solution)/shard_map/ppermute | solution.py:1245
  374.0 7.3 %shard_map.348 = bf16[1024,768]{1,0:T(8,128)(2,1)} custom-call(s32[8,1024]{1,0:T(8,128)S(1)} %copy-done.31, bf16[1024,768]{1,0:T(8,128)(2,1)} %get-tuple-element.191.refs_1_.e1, bf16[1024,768]{1,0:T(8,128)(2,1)} %get-tuple-element.198.x.refs_1_, bf16[1024,768]{1,0:T(8,128)(2,1)} %get-tuple-element.209.mine, ...), custom_call_target="tpu_custom_call" | custom-call | flops 6442450944 | bytes 37748736 | tf_op jit(solution)/shard_map/pallas_call | solution.py:1183
  383.3 5.4 %collective-permute-done.35 = bf16[192,1152]{1,0:T(8,128)(2,1)S(1)} collective-permute-done((bf16[192,1152]{1,0:T(8,128)(2,1)S(1)}, bf16[192,1152]{1,0:T(8,128)(2,1)S(1)}, u32[]{:S(2)}, u32[]{:S(2)}) %collective-permute-start.35) | collective-permute-done | bytes 442400 | tf_op jit(solution)/shard_map/ppermute | solution.py:1245
  (236 shorter events, 81.8 us)
Async XLA Ops:
  7.2 119.4 %all-gather.2.cloned.1.call-start = ((), (), s32[]{:S(2)}) async-start(), calls=%async_computation | async-start | bytes 13271040 | tf_op jit(solution)/shard_map/all_gather | solution.py:1207
  10.5 17.0 %collective-permute-start.2 = (bf16[208,1152]{1,0:T(8,128)(2,1)S(1)}, bf16[208,1152]{1,0:T(8,128)(2,1)S(1)}, u32[]{:S(2)}, u32[]{:S(2)}) collective-permute-start(bf16[208,1152]{1,0:T(8,128)(2,1)S(1)} %fusion.11.w0.refs_14_), channel_id=1, source_target_pairs={{0,4},{2,6},{4,0},{6,2},{1,5},{3,7},{5,1},{7,3},{8,12},{10,14},{12... | collective-permute-start | bytes 1437704 | tf_op jit(solution)/shard_map/ppermute | solution.py:1199
  13.5 7.4 %collective-permute-start = (bf16[208,1152]{1,0:T(8,128)(2,1)S(1)}, bf16[208,1152]{1,0:T(8,128)(2,1)S(1)}, u32[]{:S(2)}, u32[]{:S(2)}) collective-permute-start(bf16[208,1152]{1,0:T(8,128)(2,1)S(1)} %fusion.11.w0.refs_14_), channel_id=1, source_target_pairs={{0,2},{2,0},{4,6},{6,4},{1,3},{3,1},{5,7},{7,5},{8,10},{10,8},{12,... | collective-permute-start | bytes 1437704 | tf_op jit(solution)/shard_map/ppermute | solution.py:1199
  27.5 239.9 %all-reduce.3.cloned.1.call-start = ((), (), s32[]{:S(2)}) async-start(), calls=%async_computation.1 | async-start | bytes 2359296 | tf_op jit(solution)/shard_map/psum | solution.py:1402
  28.4 9.2 %collective-permute-start.4 = (bf16[192,1536]{1,0:T(8,128)(2,1)S(1)}, bf16[192,1536]{1,0:T(8,128)(2,1)S(1)}, u32[]{:S(2)}, u32[]{:S(2)}) collective-permute-start(bf16[192,1536]{1,0:T(8,128)(2,1)S(1)} %constant_dynamic-update-slice_fusion.refs_1_.refs_9_.refs_4_), channel_id=1, source_target_pairs={{0,2},{2,0},{4,6},{6,4},{1,3},{3,1},{5,7},{7,5},{8,10},{10,8},{12,... | collective-permute-start | bytes 1769480 | tf_op jit(solution)/shard_map/ppermute | solution.py:1199
  29.3 19.5 %collective-permute-start.6 = (bf16[192,384]{1,0:T(8,128)(2,1)S(1)}, bf16[192,384]{1,0:T(8,128)(2,1)S(1)}, u32[]{:S(2)}, u32[]{:S(2)}) collective-permute-start(bf16[192,384]{1,0:T(8,128)(2,1)S(1)} %collective-permute-done.1.refs_13_), channel_id=1, source_target_pairs={{0,2},{2,0},{4,6},{6,4},{1,3},{3,1},{5,7},{7,5},{8,10},{10,8},{12,... | collective-permute-start | bytes 442376 | tf_op jit(solution)/shard_map/ppermute | solution.py:1199
  29.5 13.1 %collective-permute-start.5 = (bf16[192,384]{1,0:T(8,128)(2,1)S(1)}, bf16[192,384]{1,0:T(8,128)(2,1)S(1)}, u32[]{:S(2)}, u32[]{:S(2)}) collective-permute-start(bf16[192,384]{1,0:T(8,128)(2,1)S(1)} %collective-permute-done.1.refs_13_), channel_id=1, source_target_pairs={{0,4},{2,6},{4,0},{6,2},{1,5},{3,7},{5,1},{7,3},{8,12},{10,14},{12... | collective-permute-start | bytes 442376 | tf_op jit(solution)/shard_map/ppermute | solution.py:1199
  30.0 28.7 %collective-permute-start.9 = (bf16[192,1536]{1,0:T(8,128)(2,1)S(1)}, bf16[192,1536]{1,0:T(8,128)(2,1)S(1)}, u32[]{:S(2)}, u32[]{:S(2)}) collective-permute-start(bf16[192,1536]{1,0:T(8,128)(2,1)S(1)} %constant_dynamic-update-slice_fusion.refs_1_.refs_9_.refs_4_), channel_id=1, source_target_pairs={{0,4},{2,6},{4,0},{6,2},{1,5},{3,7},{5,1},{7,3},{8,12},{10,14},{12... | collective-permute-start | bytes 1769480 | tf_op jit(solution)/shard_map/ppermute | solution.py:1199
  42.2 21.6 %collective-permute-start.8 = (bf16[1024,128]{1,0:T(8,128)(2,1)}, bf16[1024,128]{1,0:T(8,128)(2,1)S(1)}, u32[]{:S(2)}, u32[]{:S(2)}) collective-permute-start(bf16[1024,128]{1,0:T(8,128)(2,1)} %get-tuple-element.128.refs_3_.refs_6_.refs_8_), channel_id=1, source_target_pairs={{0,1},{1,0},{2,3},{3,2},{4,5},{5,4},{6,7},{7,6},{8,9},{9,8},{10,11... | collective-permute-start | bytes 786440 | tf_op jit(solution)/shard_map/ppermute | solution.py:1199
  47.1 26.0 %collective-permute-start.11 = (bf16[1024,128]{1,0:T(8,128)(2,1)}, bf16[1024,128]{1,0:T(8,128)(2,1)S(1)}, u32[]{:S(2)}, u32[]{:S(2)}) collective-permute-start(bf16[1024,128]{1,0:T(8,128)(2,1)} %get-tuple-element.130.refs_4_.refs_7_.refs_9_), channel_id=1, source_target_pairs={{0,1},{1,0},{2,3},{3,2},{4,5},{5,4},{6,7},{7,6},{8,9},{9,8},{10,11... | collective-permute-start | bytes 786440 | tf_op jit(solution)/shard_map/ppermute | solution.py:1199
  53.3 19.8 %collective-permute-start.12 = (bf16[1024,128]{1,0:T(8,128)(2,1)}, bf16[1024,128]{1,0:T(8,128)(2,1)S(1)}, u32[]{:S(2)}, u32[]{:S(2)}) collective-permute-start(bf16[1024,128]{1,0:T(8,128)(2,1)} %get-tuple-element.133.refs_5_.refs_8_.refs_10_), channel_id=1, source_target_pairs={{0,1},{1,0},{2,3},{3,2},{4,5},{5,4},{6,7},{7,6},{8,9},{9,8},{10,11... | collective-permute-start | bytes 786440 | tf_op jit(solution)/shard_map/ppermute | solution.py:1199
  92.3 15.0 %collective-permute-start.13 = (bf16[1024,128]{1,0:T(8,128)(2,1)}, bf16[1024,128]{1,0:T(8,128)(2,1)S(1)}, u32[]{:S(2)}, u32[]{:S(2)}) collective-permute-start(bf16[1024,128]{1,0:T(8,128)(2,1)} %get-tuple-element.142.refs_4_.refs_3_), channel_id=1, source_target_pairs={{0,1},{1,0},{2,3},{3,2},{4,5},{5,4},{6,7},{7,6},{8,9},{9,8},{10,11... | collective-permute-start | bytes 786440 | tf_op jit(solution)/shard_map/ppermute | solution.py:1199
  103.4 15.0 %collective-permute-start.14 = (bf16[1024,128]{1,0:T(8,128)(2,1)}, bf16[1024,128]{1,0:T(8,128)(2,1)}, u32[]{:S(2)}, u32[]{:S(2)}) collective-permute-start(bf16[1024,128]{1,0:T(8,128)(2,1)} %get-tuple-element.144.refs_5_.refs_4_), channel_id=1, source_target_pairs={{0,1},{1,0},{2,3},{3,2},{4,5},{5,4},{6,7},{7,6},{8,9},{9,8},{10,11... | collective-permute-start | bytes 786440 | tf_op jit(solution)/shard_map/ppermute | solution.py:1199
  118.3 8.3 %collective-permute-start.15 = (bf16[1024,128]{1,0:T(8,128)(2,1)}, bf16[1024,128]{1,0:T(8,128)(2,1)}, u32[]{:S(2)}, u32[]{:S(2)}) collective-permute-start(bf16[1024,128]{1,0:T(8,128)(2,1)} %get-tuple-element.146.refs_6_.refs_5_), channel_id=1, source_target_pairs={{0,1},{1,0},{2,3},{3,2},{4,5},{5,4},{6,7},{7,6},{8,9},{9,8},{10,11... | collective-permute-start | bytes 786440 | tf_op jit(solution)/shard_map/ppermute | solution.py:1199
  176.9 28.1 %collective-permute-start.17 = (bf16[192,3072]{1,0:T(8,128)(2,1)S(1)}, bf16[192,3072]{1,0:T(8,128)(2,1)S(1)}, u32[]{:S(2)}, u32[]{:S(2)}) collective-permute-start(bf16[192,3072]{1,0:T(8,128)(2,1)S(1)} %fusion.2), channel_id=1, source_target_pairs={{0,4},{2,6},{4,0},{6,2},{1,5},{3,7},{5,1},{7,3},{8,12},{10,14},{12... | collective-permute-start | bytes 3538952 | tf_op jit(solution)/shard_map/ppermute | solution.py:1199
  217.9 31.8 %collective-permute-start.18 = (bf16[1024,384]{1,0:T(8,128)(2,1)}, bf16[1024,384]{1,0:T(8,128)(2,1)S(1)}, u32[]{:S(2)}, u32[]{:S(2)}) collective-permute-start(bf16[1024,384]{1,0:T(8,128)(2,1)} %get-tuple-element.166), channel_id=1, source_target_pairs={{0,1},{1,0},{2,3},{3,2},{4,5},{5,4},{6,7},{7,6},{8,9},{9,8},{10,11... | collective-permute-start | bytes 2359304 | tf_op jit(solution)/shard_map/ppermute | solution.py:1199
  248.1 17.7 %collective-permute-start.19 = (bf16[1024,384]{1,0:T(8,128)(2,1)}, bf16[1024,384]{1,0:T(8,128)(2,1)S(1)}, u32[]{:S(2)}, u32[]{:S(2)}) collective-permute-start(bf16[1024,384]{1,0:T(8,128)(2,1)} %get-tuple-element.180.refs_2_.refs_3_), channel_id=1, source_target_pairs={{0,1},{1,0},{2,3},{3,2},{4,5},{5,4},{6,7},{7,6},{8,9},{9,8},{10,11... | collective-permute-start | bytes 2359304 | tf_op jit(solution)/shard_map/ppermute | solution.py:1199
  265.2 15.2 %collective-permute-start.20 = (bf16[2,192,1536]{2,1,0:T(8,128)(2,1)}, bf16[2,192,1536]{2,1,0:T(8,128)(2,1)}, u32[]{:S(2)}, u32[]{:S(2)}) collective-permute-start(bf16[2,192,1536]{2,1,0:T(8,128)(2,1)} %get-tuple-element.179), channel_id=1, source_target_pairs={{0,2},{2,0},{4,6},{6,4},{1,3},{3,1},{5,7},{7,5},{8,10},{10,8},{12,... | collective-permute-start | bytes 3538952 | tf_op jit(solution)/shard_map/ppermute | solution.py:1199
  265.3 51.2 %collective-permute-start.25 = (bf16[1024,384]{1,0:T(8,128)(2,1)}, bf16[1024,384]{1,0:T(8,128)(2,1)}, u32[]{:S(2)}, u32[]{:S(2)}) collective-permute-start(bf16[1024,384]{1,0:T(8,128)(2,1)} %get-tuple-element.213), channel_id=1, source_target_pairs={{0,1},{1,0},{2,3},{3,2},{4,5},{5,4},{6,7},{7,6},{8,9},{9,8},{10,11... | collective-permute-start | bytes 2359304 | tf_op jit(solution)/shard_map/ppermute | solution.py:1199
  265.8 53.8 %collective-permute-start.26 = (bf16[2048,384]{1,0:T(8,128)(2,1)}, bf16[2048,384]{1,0:T(8,128)(2,1)}, u32[]{:S(2)}, u32[]{:S(2)}) collective-permute-start(bf16[2048,384]{1,0:T(8,128)(2,1)} %get-tuple-element.217), channel_id=1, source_target_pairs={{0,1},{1,0},{2,3},{3,2},{4,5},{5,4},{6,7},{7,6},{8,9},{9,8},{10,11... | collective-permute-start | bytes 4718600 | tf_op jit(solution)/shard_map/ppermute | solution.py:1199
  281.7 16.7 %collective-permute-start.22 = (bf16[192,1536]{1,0:T(8,128)(2,1)S(1)}, bf16[192,1536]{1,0:T(8,128)(2,1)S(1)}, u32[]{:S(2)}, u32[]{:S(2)}) collective-permute-start(bf16[192,1536]{1,0:T(8,128)(2,1)S(1)} %fusion.9), channel_id=1, source_target_pairs={{0,4},{2,6},{4,0},{6,2},{1,5},{3,7},{5,1},{7,3},{8,12},{10,14},{12... | collective-permute-start | bytes 1769480 | tf_op jit(solution)/shard_map/ppermute | solution.py:1199
  298.4 7.8 %collective-permute-start.21 = (bf16[2,192,1152]{2,1,0:T(8,128)(2,1)}, bf16[2,192,1152]{2,1,0:T(8,128)(2,1)S(1)}, u32[]{:S(2)}, u32[]{:S(2)}) collective-permute-start(bf16[2,192,1152]{2,1,0:T(8,128)(2,1)} %get-tuple-element.197), channel_id=1, source_target_pairs={{0,2},{2,0},{4,6},{6,4},{1,3},{3,1},{5,7},{7,5},{8,10},{10,8},{12,... | collective-permute-start | bytes 2654216 | tf_op jit(solution)/shard_map/ppermute | solution.py:1199
  299.7 21.7 %collective-permute-start.36 = (bf16[192,1536]{1,0:T(8,128)(2,1)S(1)}, bf16[192,1536]{1,0:T(8,128)(2,1)S(1)}, u32[]{:S(2)}, u32[]{:S(2)}) collective-permute-start(bf16[192,1536]{1,0:T(8,128)(2,1)S(1)} %fusion.4), channel_id=1, source_target_pairs={{0,8},{24,16},{1,9},{25,17},{2,10},{26,18},{3,11},{27,19},{4,12},{... | collective-permute-start | bytes 1769480 | tf_op jit(solution)/shard_map/ppermute | solution.py:1232
  306.2 16.8 %collective-permute-start.23 = (bf16[192,1152]{1,0:T(8,128)(2,1)S(1)}, bf16[192,1152]{1,0:T(8,128)(2,1)S(1)}, u32[]{:S(2)}, u32[]{:S(2)}) collective-permute-start(bf16[192,1152]{1,0:T(8,128)(2,1)S(1)} %fusion.12), channel_id=1, source_target_pairs={{0,4},{2,6},{4,0},{6,2},{1,5},{3,7},{5,1},{7,3},{8,12},{10,14},{12... | collective-permute-start | bytes 1327112 | tf_op jit(solution)/shard_map/ppermute | solution.py:1199
  316.0 58.0 %collective-permute-start.24 = (bf16[1024,768]{1,0:T(8,128)(2,1)}, bf16[1024,768]{1,0:T(8,128)(2,1)S(1)}, u32[]{:S(2)}, u32[]{:S(2)}) collective-permute-start(bf16[1024,768]{1,0:T(8,128)(2,1)} %get-tuple-element.209.mine), channel_id=1, source_target_pairs={{0,1},{1,0},{2,3},{3,2},{4,5},{5,4},{6,7},{7,6},{8,9},{9,8},{10,11... | collective-permute-start | bytes 4718600 | tf_op jit(solution)/shard_map/ppermute | solution.py:1199
  321.6 27.4 %collective-permute-start.37 = (bf16[192,1536]{1,0:T(8,128)(2,1)S(1)}, bf16[192,1536]{1,0:T(8,128)(2,1)S(1)}, u32[]{:S(2)}, u32[]{:S(2)}) collective-permute-start(bf16[192,1536]{1,0:T(8,128)(2,1)S(1)} %fusion.7), channel_id=1, source_target_pairs={{8,16},{16,8},{9,17},{17,9},{10,18},{18,10},{11,19},{19,11},{12,20... | collective-permute-start | bytes 1769480 | tf_op jit(solution)/shard_map/ppermute | solution.py:1239
  322.4 14.1 %collective-permute-start.28 = (bf16[208,384]{1,0:T(8,128)(2,1)S(1)}, bf16[208,384]{1,0:T(8,128)(2,1)S(1)}, u32[]{:S(2)}, u32[]{:S(2)}) collective-permute-start(bf16[208,384]{1,0:T(8,128)(2,1)S(1)} %fusion.17), channel_id=1, source_target_pairs={{0,4},{2,6},{4,0},{6,2},{1,5},{3,7},{5,1},{7,3},{8,12},{10,14},{12... | collective-permute-start | bytes 479240 | tf_op jit(solution)/shard_map/ppermute | solution.py:1199
  323.2 21.1 %collective-permute-start.30 = (bf16[192,1152]{1,0:T(8,128)(2,1)S(1)}, bf16[192,1152]{1,0:T(8,128)(2,1)S(1)}, u32[]{:S(2)}, u32[]{:S(2)}) collective-permute-start(bf16[192,1152]{1,0:T(8,128)(2,1)S(1)} %fusion.6), channel_id=1, source_target_pairs={{0,8},{24,16},{1,9},{25,17},{2,10},{26,18},{3,11},{27,19},{4,12},{... | collective-permute-start | bytes 1327112 | tf_op jit(solution)/shard_map/ppermute | solution.py:1232
  336.6 7.7 %collective-permute-start.29 = (bf16[208,384]{1,0:T(8,128)(2,1)S(1)}, bf16[208,384]{1,0:T(8,128)(2,1)S(1)}, u32[]{:S(2)}, u32[]{:S(2)}) collective-permute-start(bf16[208,384]{1,0:T(8,128)(2,1)S(1)} %fusion.14), channel_id=1, source_target_pairs={{0,8},{24,16},{1,9},{25,17},{2,10},{26,18},{3,11},{27,19},{4,12},{... | collective-permute-start | bytes 479240 | tf_op jit(solution)/shard_map/ppermute | solution.py:1232
  347.8 21.8 %collective-permute-start.33 = (bf16[208,384]{1,0:T(8,128)(2,1)S(1)}, bf16[208,384]{1,0:T(8,128)(2,1)S(1)}, u32[]{:S(2)}, u32[]{:S(2)}) collective-permute-start(bf16[208,384]{1,0:T(8,128)(2,1)S(1)} %add_convert_fusion.12), channel_id=1, source_target_pairs={{8,0},{16,24},{9,1},{17,25},{10,2},{18,26},{11,3},{19,27},{12,4},{... | collective-permute-start | bytes 479240 | tf_op jit(solution)/shard_map/ppermute | solution.py:1245
  349.2 33.0 %collective-permute-start.38 = (bf16[192,1536]{1,0:T(8,128)(2,1)S(1)}, bf16[192,1536]{1,0:T(8,128)(2,1)S(1)}, u32[]{:S(2)}, u32[]{:S(2)}) collective-permute-start(bf16[192,1536]{1,0:T(8,128)(2,1)S(1)} %add_convert_fusion.4), channel_id=1, source_target_pairs={{8,0},{16,24},{9,1},{17,25},{10,2},{18,26},{11,3},{19,27},{12,4},{... | collective-permute-start | bytes 1769480 | tf_op jit(solution)/shard_map/ppermute | solution.py:1245
  350.5 38.2 %collective-permute-start.35 = (bf16[192,1152]{1,0:T(8,128)(2,1)S(1)}, bf16[192,1152]{1,0:T(8,128)(2,1)S(1)}, u32[]{:S(2)}, u32[]{:S(2)}) collective-permute-start(bf16[192,1152]{1,0:T(8,128)(2,1)S(1)} %add_convert_fusion.8), channel_id=1, source_target_pairs={{8,0},{16,24},{9,1},{17,25},{10,2},{18,26},{11,3},{19,27},{12,4},{... | collective-permute-start | bytes 1327112 | tf_op jit(solution)/shard_map/ppermute | solution.py:1245
  (61 other events, 790.2 us)
Sparse Core Ops, SparseCore 0:
  27.6 86.7 all-gather.1
  206.7 57.6 all-reduce.2

commit v2 on v1

--- a/solution.py
+++ b/solution.py
@@ -189,7 +189,7 @@
 def restore_kernel(pos, values, out):
     count = values.shape[0]
     onehot = (
-        lax.broadcasted_iota(jnp.int32, (count, TILE), 0) == pos[0:1, :]
+        lax.broadcasted_iota(jnp.int32, (count, ROWS), 0) == pos[0:1, :]
     ).astype(F32).astype(BF16)
     out[...] = dot(onehot, values[...], TN).astype(BF16)
 
@@ -198,9 +198,9 @@
     count, width = values.shape
     return pl.pallas_call(
         restore_kernel,
-        grid=(count // TILE,),
-        in_specs=[pl.BlockSpec((8, TILE), lambda t: (0, t)), whole((count, width))],
-        out_specs=rows(width, TILE),
+        grid=(count // ROWS,),
+        in_specs=[pl.BlockSpec((8, ROWS), lambda t: (0, t)), whole((count, width))],
+        out_specs=rows(width, ROWS),
         out_shape=shape_of((count, width), BF16),
         compiler_params=params(),
         cost_estimate=cost(2 * count * count * width, 4 * count * width),
@@ -1171,7 +1171,7 @@
 
 def last_step(pos, e1, x, mine, theirs, gain):
     count, width = x.shape
-    steps = count // TILE
+    steps = count // ROWS
 
     def early(t):
         return (jnp.minimum(t, steps - 1), 0)
@@ -1179,14 +1179,14 @@
     def late(t):
         return jnp.maximum(t - steps, 0)
 
-    tile = pl.BlockSpec((TILE, width), early)
+    tile = pl.BlockSpec((ROWS, width), early)
     return pl.pallas_call(
         last_kernel,
         grid=(2 * steps,),
-        in_specs=[pl.BlockSpec((8, TILE), lambda t: (0, late(t)))]
+        in_specs=[pl.BlockSpec((8, ROWS), lambda t: (0, late(t)))]
         + [tile] * 4
         + [whole((1, width))],
-        out_specs=pl.BlockSpec((TILE, width), lambda t: (late(t), 0)),
+        out_specs=pl.BlockSpec((ROWS, width), lambda t: (late(t), 0)),
         out_shape=shape_of((count, width), BF16),
         scratch_shapes=[pltpu.VMEM((count, width), BF16)],
         compiler_params=params(),
@@ -1488,12 +1488,9 @@
     tokens_grad = last_step(pos, e1, x, dn1, dn1_theirs, all_gains[0])
     memory_grad = jnp.stack([after(memory0, self_part), memory1])
     cross_sum = line_third(line_second(cross_part), tokens_grad)
-    self_first = line_first(self_part)
-    self_second = line_second(self_first)
+    self_second = line_second(line_first(self_part))
     self_sum = line_third(self_second, tokens_grad)
-    last_first = after(line_first(last_part), self_first)
-    last_second = after(line_second(last_first), self_second)
-    last_sum = line_third(last_second)
+    last_sum = line_third(line_second(line_first(last_part)))
     gain_sums = last_sum[share:, :share].astype(F32)
     first_gain = gain_sums[0] + swap(after(gain_sums, self_second), "narrow", 1)[0]
 

time: 404 us -> 396 us (0.980)
  waiting for transfers between devices: 59 us -> 49.1 us
    ppermute x3, waiting for transfers between devices: 24.1 us -> 16.2 us  [line_third(): got = after(lax.ppermute(values, 'dp', [(1, 0), (2, 3)]), *others)]
  transfers between devices with their start and end apart: 41 -> 41, of which waited for: 11 -> 10; matrix products, arithmetic and copies ran while one was open for 5% -> 5% of each run, Pallas kernels for 52% -> 53%
where the time goes in v2:
time: 396 us; the launch traced here: 390 us
  Pallas kernels  249 us (63%)
  waiting for transfers between devices  49.1 us (12%)
  starting transfers between devices  42.2 us (11%)
  other arithmetic  19.9 us (5%)
  between operations  15.3 us (4%)
  local copies, waits for them, and re-layouts  15.2 us (4%)
    pallas_call x2, Pallas kernels, cross_backward(): pl.pallas_call(second_kernel if image else first_kernel, grid_spec=pltpu....  50.8 us
    pallas_call x3, Pallas kernels, cross_forward(): pl.pallas_call(cross_forward_kernel, grid_spec=pltpu.PrefetchScalarGridSp...  33.3 us
    pallas_call x1, Pallas kernels, units_step(): pl.pallas_call(kernel, grid=(count // ROWS,), in_specs=[SCALARS, rows(wid...  33 us
    ppermute x30, waiting for transfers between devices, swap(): return lax.ppermute(values, axis, [(i, i ^ distance) for i in range(size)])  27.3 us
    pallas_call x3, Pallas kernels, weight_grads(): pl.pallas_call(kernel, grid=(len(plan),), in_specs=[SCALARS] + [ANY] * (l...  23.3 us
    ppermute x30, starting transfers between devices, swap(): return lax.ppermute(values, axis, [(i, i ^ distance) for i in range(size)])  22.1 us
    pallas_call x2, Pallas kernels, memory_back(): pl.pallas_call(kernel, grid=(steps,), in_specs=[SCALARS, pl.BlockSpec((BA...  18.8 us
    ppermute x3, waiting for transfers between devices, line_third(): got = after(lax.ppermute(values, 'dp', [(1, 0), (2, 3)]), *others)  16.2 us
  transfers between devices with their start and end apart: 41, of which 10 were waited for; matrix products, arithmetic and copies ran while one was open for 5% of the time, Pallas kernels for 53%

profile of v2, /device:TPU:0, one launch (start us, length us, event | category | flops | bytes accessed | tf_op | source)
XLA Modules:
  0.0 390.3 jit_solution(9265934689179403615)
XLA Ops:
  20.9 5.8 %shard_map.323 = (bf16[1024,768]{1,0:T(8,128)(2,1)}, f32[8,1024]{1,0:T(8,128)S(1)}, f32[1024,128]{1,0:T(8,128)S(1)}, s32[8,1024]{1,0:T(8,128)S(1)}, s32[32]{0:T(128)S(1)}) custom-call(s32[1,1024]{1,0:T(1,128)S(1)} %copy-done.17, s32[1,1024]{1,0:T(1,128)S(1)} %copy-done.18, s32[1,8]{1,0:T(1,128)S(1)} %copy-done.19, bf16[1024,768]{1,0:T(8,128)(2,1)} %x.2), custom_call_target="tpu_custom_call" | custom-call | flops 6442450944 | bytes 25165824 | tf_op jit(solution)/shard_map/pallas_call | solution.py:140
  32.3 5.3 %shard_map.324 = (bf16[1024,768]{1,0:T(8,128)(2,1)}, bf16[1024,1152]{1,0:T(8,128)(2,1)S(1)}) custom-call(s32[5]{0:T(128)S(1)} %stack.65.places.refs_0_, bf16[1024,768]{1,0:T(8,128)(2,1)} %get-tuple-element.196.x.refs_1_, f32[1,768]{1,0:T(1,128)S(1)} %get-tuple-element.247.gain, bf16[208,1152]{1,0:T(8,128)(2,1)S(1)} %fusion.11.w0.refs_14_, ...), custom_call_target="tpu_custom_call" | custom-call | flops 7247757312 | bytes 22020096 | tf_op jit(solution)/shard_map/pallas_call | solution.py:259
  37.7 4.5 %shard_map.325 = (bf16[1024,128]{1,0:T(8,128)(2,1)}, f32[8,1024]{1,0:T(8,128)}) custom-call(bf16[1024,1152]{1,0:T(8,128)(2,1)S(1)} %get-tuple-element.130.q.k.v, bf16[1024,1152]{1,0:T(8,128)(2,1)S(1)} %get-tuple-element.130.q.k.v, bf16[1024,1152]{1,0:T(8,128)(2,1)S(1)} %get-tuple-element.130.q.k.v, f32[8,1024]{1,0:T(8,128)S(1)} %get-tuple-element.124.row_ids, ...), custom_call_target="tpu_custom_call" | custom-call | flops 5368709120 | bytes 4194304 | tf_op jit(solution)/shard_map/pallas_call | solution.py:351
  42.6 4.5 %shard_map.326 = (bf16[1024,128]{1,0:T(8,128)(2,1)}, f32[8,1024]{1,0:T(8,128)}) custom-call(bf16[1024,1152]{1,0:T(8,128)(2,1)S(1)} %get-tuple-element.130.q.k.v, bf16[1024,1152]{1,0:T(8,128)(2,1)S(1)} %get-tuple-element.130.q.k.v, bf16[1024,1152]{1,0:T(8,128)(2,1)S(1)} %get-tuple-element.130.q.k.v, f32[8,1024]{1,0:T(8,128)S(1)} %get-tuple-element.124.row_ids, ...), custom_call_target="tpu_custom_call" | custom-call | flops 5368709120 | bytes 4194304 | tf_op jit(solution)/shard_map/pallas_call | solution.py:351
  53.7 5.0 %collective-permute-done.9.refs_2_.refs_10_.refs_5_ = bf16[192,1536]{1,0:T(8,128)(2,1)S(1)} collective-permute-done((bf16[192,1536]{1,0:T(8,128)(2,1)S(1)}, bf16[192,1536]{1,0:T(8,128)(2,1)S(1)}, u32[]{:S(2)}, u32[]{:S(2)}) %collective-permute-start.9) | collective-permute-done | bytes 589856 | tf_op jit(solution)/shard_map/ppermute | solution.py:1199
  58.8 5.3 %shard_map.328.refs_3_.refs_1_ = bf16[1024,768]{1,0:T(8,128)(2,1)} custom-call(s32[8,1024]{1,0:T(8,128)S(1)} %get-tuple-element.120.pos, bf16[1024,768]{1,0:T(8,128)(2,1)} %values), custom_call_target="tpu_custom_call" | custom-call | flops 6442450944 | bytes 12582912 | tf_op jit(solution)/shard_map/pallas_call | solution.py:178
  64.1 9.5 %shard_map.329.k.v.refs_2_.refs_3_ = bf16[4096,768]{1,0:T(8,128)(2,1)} custom-call(s32[5]{0:T(128)S(1)} %stack.65.places.refs_0_, bf16[4096,768]{1,0:T(8,128)(2,1)} %bitcast.55, bf16[192,1536]{1,0:T(8,128)(2,1)S(1)} %constant_dynamic-update-slice_fusion.refs_1_.refs_9_.refs_4_, bf16[192,1536]{1,0:T(8,128)(2,1)S(1)} %collective-permute-done.9.refs_2_.refs_10_.refs_5_, ...), custom_call_target="tpu_custom_call" | custom-call | flops 19327352832 | bytes 50331648 | tf_op jit(solution)/shard_map/pallas_call | solution.py:292
  73.6 7.9 %shard_map.330 = (bf16[1024,768]{1,0:T(8,128)(2,1)}, bf16[1024,768]{1,0:T(8,128)(2,1)}, bf16[1024,384]{1,0:T(8,128)(2,1)}) custom-call(s32[5]{0:T(128)S(1)} %stack.65.places.refs_0_, bf16[1024,768]{1,0:T(8,128)(2,1)} %get-tuple-element.196.x.refs_1_, f32[1,768]{1,0:T(1,128)S(1)} %get-tuple-element.246.refs_2_.refs_5_, ...), custom_call_target="tpu_custom_call" | custom-call | flops 7247757312 | bytes 37748736 | tf_op jit(solution)/shard_map/pallas_call | solution.py:839
  81.6 11.1 %shard_map.331 = (bf16[1024,128]{1,0:T(8,128)(2,1)}, f32[8,1024]{1,0:T(8,128)}) custom-call(s32[32]{0:T(128)S(1)} %get-tuple-element.138.scalars.refs_0_, bf16[1024,384]{1,0:T(8,128)(2,1)} %get-tuple-element.143.q.refs_1_, bf16[4096,768]{1,0:T(8,128)(2,1)} %shard_map.329.k.v.refs_2_.refs_3_, bf16[4096,768]{1,0:T(8,128)(2,1)} %shard_map.329.k.v.refs_2_.refs_3_), custom_call_target="tpu_custom_call" | custom-call | flops 21474836480 | bytes 8388608 | tf_op jit(solution)/shard_map/pallas_call | solution.py:483
  92.7 11.1 %shard_map.332 = (bf16[1024,128]{1,0:T(8,128)(2,1)}, f32[8,1024]{1,0:T(8,128)}) custom-call(s32[32]{0:T(128)S(1)} %get-tuple-element.138.scalars.refs_0_, bf16[1024,384]{1,0:T(8,128)(2,1)} %get-tuple-element.143.q.refs_1_, bf16[4096,768]{1,0:T(8,128)(2,1)} %shard_map.329.k.v.refs_2_.refs_3_, bf16[4096,768]{1,0:T(8,128)(2,1)} %shard_map.329.k.v.refs_2_.refs_3_), custom_call_target="tpu_custom_call" | custom-call | flops 21474836480 | bytes 8388608 | tf_op jit(solution)/shard_map/pallas_call | solution.py:483
  107.7 11.1 %shard_map.333 = (bf16[1024,128]{1,0:T(8,128)(2,1)}, f32[8,1024]{1,0:T(8,128)}) custom-call(s32[32]{0:T(128)S(1)} %get-tuple-element.138.scalars.refs_0_, bf16[1024,384]{1,0:T(8,128)(2,1)} %get-tuple-element.143.q.refs_1_, bf16[4096,768]{1,0:T(8,128)(2,1)} %shard_map.329.k.v.refs_2_.refs_3_, bf16[4096,768]{1,0:T(8,128)(2,1)} %shard_map.329.k.v.refs_2_.refs_3_), custom_call_target="tpu_custom_call" | custom-call | flops 21474836480 | bytes 8388608 | tf_op jit(solution)/shard_map/pallas_call | solution.py:483
  118.8 8.1 %collective-permute-done.15.refs_9_ = bf16[1024,128]{1,0:T(8,128)(2,1)} collective-permute-done((bf16[1024,128]{1,0:T(8,128)(2,1)}, bf16[1024,128]{1,0:T(8,128)(2,1)}, u32[]{:S(2)}, u32[]{:S(2)}) %collective-permute-start.15) | collective-permute-done | bytes 262176 | tf_op jit(solution)/shard_map/ppermute | solution.py:1199
  126.9 33.0 %shard_map.334 = (bf16[1024,768]{1,0:T(8,128)(2,1)}, bf16[1024,768]{1,0:T(8,128)(2,1)}, bf16[1024,1024]{1,0:T(8,128)(2,1)}, bf16[1024,1024]{1,0:T(8,128)(2,1)}, ...) custom-call(s32[5]{0:T(128)} %copy-done.4, ...), custom_call_target="tpu_custom_call" | custom-call | flops 96636764160 | bytes 94371840 | tf_op jit(solution)/shard_map/pallas_call | solution.py:970
  160.0 10.3 %shard_map.335 = (bf16[2,192,3072]{2,1,0:T(8,128)(2,1)}, bf16[2,192,3072]{2,1,0:T(8,128)(2,1)}) custom-call(s32[5]{0:T(128)S(1)} %copy-done.5, bf16[1024,768]{1,0:T(8,128)(2,1)} %get-tuple-element.150.refs_0_, bf16[1024,768]{1,0:T(8,128)(2,1)} %shard_map.328.refs_3_.refs_1_, bf16[1024,1024]{1,0:T(8,128)(2,1)} %get-tuple-element.151.refs_2_, ...), custom_call_target="tpu_custom_call" | custom-call | flops 19327352832 | bytes 37748736 | tf_op jit(solution)/shard_map/pallas_call | solution.py:781
  170.4 4.7 %collective-permute-done.16 = bf16[2,192,3072]{2,1,0:T(8,128)(2,1)S(1)} collective-permute-done((bf16[2,192,3072]{2,1,0:T(8,128)(2,1)}, bf16[2,192,3072]{2,1,0:T(8,128)(2,1)S(1)}, u32[]{:S(2)}, u32[]{:S(2)}) %collective-permute-start.16) | collective-permute-done | bytes 2359328 | tf_op jit(solution)/shard_map/ppermute | solution.py:1199
  177.3 38.5 %shard_map.336 = (bf16[1024,384]{1,0:T(8,128)(2,1)}, bf16[2048,384]{1,0:T(8,128)(2,1)}, bf16[2048,384]{1,0:T(8,128)(2,1)}) custom-call(s32[32]{0:T(128)S(1)} %get-tuple-element.138.scalars.refs_0_, bf16[1024,384]{1,0:T(8,128)(2,1)} %get-tuple-element.143.q.refs_1_, bf16[4096,768]{1,0:T(8,128)(2,1)} %shard_map.329.k.v.refs_2_.refs_3_, ...), custom_call_target="tpu_custom_call" | custom-call | flops 80530636800 | bytes 25165824 | tf_op jit(solution)/shard_map/pallas_call | solution.py:571
  219.7 9.3 %shard_map.337 = (bf16[2048,384]{1,0:T(8,128)(2,1)}, bf16[1024,384]{1,0:T(8,128)(2,1)}, bf16[1024,384]{1,0:T(8,128)(2,1)}, f32[768,768]{1,0:T(8,128)S(1)}) custom-call(s32[5]{0:T(128)S(1)} %copy-done.5, bf16[4096,768]{1,0:T(8,128)(2,1)} %bitcast.56, bf16[2048,384]{1,0:T(8,128)(2,1)} %get-tuple-element.162.refs_2_, ...), custom_call_target="tpu_custom_call" | custom-call | flops 19327352832 | bytes 50331648 | tf_op jit(solution)/shard_map/pallas_call | solution.py:652
  229.5 12.3 %shard_map.338 = (bf16[1024,384]{1,0:T(8,128)(2,1)}, bf16[2048,384]{1,0:T(8,128)(2,1)}, bf16[2048,384]{1,0:T(8,128)(2,1)}) custom-call(s32[32]{0:T(128)S(1)} %get-tuple-element.138.scalars.refs_0_, bf16[1024,384]{1,0:T(8,128)(2,1)} %get-tuple-element.143.q.refs_1_, bf16[4096,768]{1,0:T(8,128)(2,1)} %shard_map.329.k.v.refs_2_.refs_3_, ...), custom_call_target="tpu_custom_call" | custom-call | flops 80530636800 | bytes 25165824 | tf_op jit(solution)/shard_map/pallas_call | solution.py:571
  243.5 6.3 %collective-permute-done.18 = bf16[1024,384]{1,0:T(8,128)(2,1)S(1)} collective-permute-done((bf16[1024,384]{1,0:T(8,128)(2,1)}, bf16[1024,384]{1,0:T(8,128)(2,1)S(1)}, u32[]{:S(2)}, u32[]{:S(2)}) %collective-permute-start.18) | collective-permute-done | bytes 786464 | tf_op jit(solution)/shard_map/ppermute | solution.py:1199
  249.8 9.4 %shard_map.339 = (bf16[2048,384]{1,0:T(8,128)(2,1)}, bf16[2048,384]{1,0:T(8,128)(2,1)}, bf16[2,192,1536]{2,1,0:T(8,128)(2,1)}, bf16[2,192,1536]{2,1,0:T(8,128)(2,1)}) custom-call(s32[5]{0:T(128)S(1)} %copy-done.5, bf16[4096,768]{1,0:T(8,128)(2,1)} %bitcast.57, bf16[2048,384]{1,0:T(8,128)(2,1)} %get-tuple-element.170.refs_2_, ...), custom_call_target="tpu_custom_call" | custom-call | flops 19327352832 | bytes 50331648 | tf_op jit(solution)/shard_map/pallas_call | solution.py:652
  259.3 6.0 %shard_map.340 = (bf16[2,192,1536]{2,1,0:T(8,128)(2,1)}, bf16[2,192,1536]{2,1,0:T(8,128)(2,1)}) custom-call(s32[5]{0:T(128)S(1)} %copy-done.5, bf16[1024,768]{1,0:T(8,128)(2,1)} %get-tuple-element.174.refs_0_, bf16[1024,768]{1,0:T(8,128)(2,1)} %get-tuple-element.148.refs_1_, ...), custom_call_target="tpu_custom_call", output_to_operand_aliasing={{0}: (7, {}), {1}: (8, {})} | custom-call | flops 4831838208 | bytes 25165824 | tf_op jit(solution)/shard_map/pallas_call | solution.py:781
  272.9 9.8 %shard_map.341 = (bf16[1024,768]{1,0:T(8,128)(2,1)}, bf16[1024,384]{1,0:T(8,128)(2,1)S(1)}, f32[24,1024]{1,0:T(8,128)S(1)}, f32[8,768]{1,0:T(8,128)S(1)}) custom-call(s32[5]{0:T(128)S(1)} %copy-done.5, bf16[1024,768]{1,0:T(8,128)(2,1)} %get-tuple-element.148.refs_1_, bf16[1024,768]{1,0:T(8,128)(2,1)} %get-tuple-element.137.refs_1_.refs_2_, ...), custom_call_target="tpu_custom_call" | custom-call | flops 7247757312 | bytes 50331648 | tf_op jit(solution)/shard_map/pallas_call | solution.py:1045
  285.6 4.5 %shard_map.342 = (bf16[1024,128]{1,0:T(8,128)(2,1)}, bf16[1024,128]{1,0:T(8,128)(2,1)}, bf16[1024,128]{1,0:T(8,128)(2,1)}) custom-call(bf16[1024,1152]{1,0:T(8,128)(2,1)S(1)} %copy-done.21, bf16[1024,1152]{1,0:T(8,128)(2,1)S(1)} %copy-done.21, bf16[1024,1152]{1,0:T(8,128)(2,1)S(1)} %copy-done.21, bf16[1024,384]{1,0:T(8,128)(2,1)S(1)} %get-tuple-element.200.grad, ...), custom_call_target="tpu_custom_call" | custom-call | flops 13421772800 | bytes 8388608 | tf_op jit(solution)/shard_map/pallas_call | solution.py:404
  290.1 4.5 %shard_map.343 = (bf16[1024,128]{1,0:T(8,128)(2,1)}, bf16[1024,128]{1,0:T(8,128)(2,1)}, bf16[1024,128]{1,0:T(8,128)(2,1)}) custom-call(bf16[1024,1152]{1,0:T(8,128)(2,1)S(1)} %copy-done.21, bf16[1024,1152]{1,0:T(8,128)(2,1)S(1)} %copy-done.21, bf16[1024,1152]{1,0:T(8,128)(2,1)S(1)} %copy-done.21, bf16[1024,384]{1,0:T(8,128)(2,1)S(1)} %get-tuple-element.200.grad, ...), custom_call_target="tpu_custom_call" | custom-call | flops 13421772800 | bytes 8388608 | tf_op jit(solution)/shard_map/pallas_call | solution.py:404
  294.7 7.0 %shard_map.344 = (bf16[2,192,1152]{2,1,0:T(8,128)(2,1)}, bf16[2,192,1152]{2,1,0:T(8,128)(2,1)}) custom-call(s32[5]{0:T(128)S(1)} %copy-done.5, bf16[1024,768]{1,0:T(8,128)(2,1)} %get-tuple-element.188.refs_0_.refs_2_, bf16[1024,768]{1,0:T(8,128)(2,1)} %get-tuple-element.189.refs_1_.e1, bf16[1024,128]{1,0:T(8,128)(2,1)} %get-tuple-element.184.refs_2_.refs_5_, ...), custom_call_target="tpu_custom_call" | custom-call | flops 7247757312 | bytes 25165824 | tf_op jit(solution)/shard_map/pallas_call | solution.py:781
  303.1 7.8 %collective-permute-start.36 = (bf16[192,1536]{1,0:T(8,128)(2,1)S(1)}, bf16[192,1536]{1,0:T(8,128)(2,1)S(1)}, u32[]{:S(2)}, u32[]{:S(2)}) collective-permute-start(bf16[192,1536]{1,0:T(8,128)(2,1)S(1)} %fusion.4), channel_id=1, source_target_pairs={{0,8},{24,16},{1,9},{25,17},{2,10},{26,18},{3,11},{27,19},{4,12},{... | collective-permute-start | bytes 1769480 | tf_op jit(solution)/shard_map/ppermute | solution.py:1232
  310.9 4.6 %shard_map.345 = (bf16[1024,128]{1,0:T(8,128)(2,1)}, bf16[1024,128]{1,0:T(8,128)(2,1)}, bf16[1024,128]{1,0:T(8,128)(2,1)}) custom-call(bf16[1024,1152]{1,0:T(8,128)(2,1)S(1)} %copy-done.21, bf16[1024,1152]{1,0:T(8,128)(2,1)S(1)} %copy-done.21, bf16[1024,1152]{1,0:T(8,128)(2,1)S(1)} %copy-done.21, bf16[1024,384]{1,0:T(8,128)(2,1)S(1)} %get-tuple-element.200.grad, ...), custom_call_target="tpu_custom_call" | custom-call | flops 13421772800 | bytes 8388608 | tf_op jit(solution)/shard_map/pallas_call | solution.py:404
  315.7 7.7 %shard_map.346 = (bf16[1024,768]{1,0:T(8,128)(2,1)}, bf16[2,208,384]{2,1,0:T(8,128)(2,1)S(1)}, bf16[2,208,384]{2,1,0:T(8,128)(2,1)S(1)}) custom-call(s32[5]{0:T(128)S(1)} %copy-done.5, bf16[1024,768]{1,0:T(8,128)(2,1)} %get-tuple-element.196.x.refs_1_, bf16[1024,768]{1,0:T(8,128)(2,1)} %get-tuple-element.188.refs_0_.refs_2_, ...), custom_call_target="tpu_custom_call" | custom-call | flops 9663676416 | bytes 25165824 | tf_op jit(solution)/shard_map/pallas_call | solution.py:1128
  330.6 4.7 %collective-permute-start.32 = (bf16[192,1152]{1,0:T(8,128)(2,1)S(1)}, bf16[192,1152]{1,0:T(8,128)(2,1)S(1)}, u32[]{:S(2)}, u32[]{:S(2)}) collective-permute-start(bf16[192,1152]{1,0:T(8,128)(2,1)S(1)} %fusion.6), channel_id=1, source_target_pairs={{0,8},{24,16},{1,9},{25,17},{2,10},{26,18},{3,11},{27,19},{4,12},{... | collective-permute-start | bytes 1327112 | tf_op jit(solution)/shard_map/ppermute | solution.py:1232
  352.6 10.2 %collective-permute-done.31 = bf16[208,384]{1,0:T(8,128)(2,1)S(1)} collective-permute-done((bf16[208,384]{1,0:T(8,128)(2,1)S(1)}, bf16[208,384]{1,0:T(8,128)(2,1)S(1)}, u32[]{:S(2)}, u32[]{:S(2)}) %collective-permute-start.31) | collective-permute-done | bytes 159776 | tf_op jit(solution)/shard_map/ppermute | solution.py:1245
  367.3 6.3 %shard_map.348 = bf16[1024,768]{1,0:T(8,128)(2,1)} custom-call(s32[8,1024]{1,0:T(8,128)S(1)} %copy-done.31, bf16[1024,768]{1,0:T(8,128)(2,1)} %get-tuple-element.189.refs_1_.e1, bf16[1024,768]{1,0:T(8,128)(2,1)} %get-tuple-element.196.x.refs_1_, bf16[1024,768]{1,0:T(8,128)(2,1)} %get-tuple-element.207.mine, ...), custom_call_target="tpu_custom_call" | custom-call | flops 6442450944 | bytes 37748736 | tf_op jit(solution)/shard_map/pallas_call | solution.py:1183
  374.7 6.0 %collective-permute-done.35 = bf16[192,1152]{1,0:T(8,128)(2,1)S(1)} collective-permute-done((bf16[192,1152]{1,0:T(8,128)(2,1)S(1)}, bf16[192,1152]{1,0:T(8,128)(2,1)S(1)}, u32[]{:S(2)}, u32[]{:S(2)}) %collective-permute-start.35) | collective-permute-done | bytes 442400 | tf_op jit(solution)/shard_map/ppermute | solution.py:1245
  (236 shorter events, 82.5 us)
Async XLA Ops:
  7.2 119.7 %all-gather.2.cloned.1.call-start = ((), (), s32[]{:S(2)}) async-start(), calls=%async_computation | async-start | bytes 13271040 | tf_op jit(solution)/shard_map/all_gather | solution.py:1207
  10.5 17.0 %collective-permute-start.2 = (bf16[208,1152]{1,0:T(8,128)(2,1)S(1)}, bf16[208,1152]{1,0:T(8,128)(2,1)S(1)}, u32[]{:S(2)}, u32[]{:S(2)}) collective-permute-start(bf16[208,1152]{1,0:T(8,128)(2,1)S(1)} %fusion.11.w0.refs_14_), channel_id=1, source_target_pairs={{0,4},{2,6},{4,0},{6,2},{1,5},{3,7},{5,1},{7,3},{8,12},{10,14},{12... | collective-permute-start | bytes 1437704 | tf_op jit(solution)/shard_map/ppermute | solution.py:1199
  13.5 7.4 %collective-permute-start = (bf16[208,1152]{1,0:T(8,128)(2,1)S(1)}, bf16[208,1152]{1,0:T(8,128)(2,1)S(1)}, u32[]{:S(2)}, u32[]{:S(2)}) collective-permute-start(bf16[208,1152]{1,0:T(8,128)(2,1)S(1)} %fusion.11.w0.refs_14_), channel_id=1, source_target_pairs={{0,2},{2,0},{4,6},{6,4},{1,3},{3,1},{5,7},{7,5},{8,10},{10,8},{12,... | collective-permute-start | bytes 1437704 | tf_op jit(solution)/shard_map/ppermute | solution.py:1199
  27.5 242.2 %all-reduce.3.cloned.1.call-start = ((), (), s32[]{:S(2)}) async-start(), calls=%async_computation.1 | async-start | bytes 2359296 | tf_op jit(solution)/shard_map/psum | solution.py:1402
  28.4 9.3 %collective-permute-start.4 = (bf16[192,1536]{1,0:T(8,128)(2,1)S(1)}, bf16[192,1536]{1,0:T(8,128)(2,1)S(1)}, u32[]{:S(2)}, u32[]{:S(2)}) collective-permute-start(bf16[192,1536]{1,0:T(8,128)(2,1)S(1)} %constant_dynamic-update-slice_fusion.refs_1_.refs_9_.refs_4_), channel_id=1, source_target_pairs={{0,2},{2,0},{4,6},{6,4},{1,3},{3,1},{5,7},{7,5},{8,10},{10,8},{12,... | collective-permute-start | bytes 1769480 | tf_op jit(solution)/shard_map/ppermute | solution.py:1199
  29.3 19.6 %collective-permute-start.6 = (bf16[192,384]{1,0:T(8,128)(2,1)S(1)}, bf16[192,384]{1,0:T(8,128)(2,1)S(1)}, u32[]{:S(2)}, u32[]{:S(2)}) collective-permute-start(bf16[192,384]{1,0:T(8,128)(2,1)S(1)} %collective-permute-done.1.refs_13_), channel_id=1, source_target_pairs={{0,2},{2,0},{4,6},{6,4},{1,3},{3,1},{5,7},{7,5},{8,10},{10,8},{12,... | collective-permute-start | bytes 442376 | tf_op jit(solution)/shard_map/ppermute | solution.py:1199
  29.5 13.1 %collective-permute-start.5 = (bf16[192,384]{1,0:T(8,128)(2,1)S(1)}, bf16[192,384]{1,0:T(8,128)(2,1)S(1)}, u32[]{:S(2)}, u32[]{:S(2)}) collective-permute-start(bf16[192,384]{1,0:T(8,128)(2,1)S(1)} %collective-permute-done.1.refs_13_), channel_id=1, source_target_pairs={{0,4},{2,6},{4,0},{6,2},{1,5},{3,7},{5,1},{7,3},{8,12},{10,14},{12... | collective-permute-start | bytes 442376 | tf_op jit(solution)/shard_map/ppermute | solution.py:1199
  30.0 28.8 %collective-permute-start.9 = (bf16[192,1536]{1,0:T(8,128)(2,1)S(1)}, bf16[192,1536]{1,0:T(8,128)(2,1)S(1)}, u32[]{:S(2)}, u32[]{:S(2)}) collective-permute-start(bf16[192,1536]{1,0:T(8,128)(2,1)S(1)} %constant_dynamic-update-slice_fusion.refs_1_.refs_9_.refs_4_), channel_id=1, source_target_pairs={{0,4},{2,6},{4,0},{6,2},{1,5},{3,7},{5,1},{7,3},{8,12},{10,14},{12... | collective-permute-start | bytes 1769480 | tf_op jit(solution)/shard_map/ppermute | solution.py:1199
  42.2 21.8 %collective-permute-start.8 = (bf16[1024,128]{1,0:T(8,128)(2,1)}, bf16[1024,128]{1,0:T(8,128)(2,1)S(1)}, u32[]{:S(2)}, u32[]{:S(2)}) collective-permute-start(bf16[1024,128]{1,0:T(8,128)(2,1)} %get-tuple-element.126.refs_3_.refs_6_.refs_8_), channel_id=1, source_target_pairs={{0,1},{1,0},{2,3},{3,2},{4,5},{5,4},{6,7},{7,6},{8,9},{9,8},{10,11... | collective-permute-start | bytes 786440 | tf_op jit(solution)/shard_map/ppermute | solution.py:1199
  47.2 26.4 %collective-permute-start.11 = (bf16[1024,128]{1,0:T(8,128)(2,1)}, bf16[1024,128]{1,0:T(8,128)(2,1)S(1)}, u32[]{:S(2)}, u32[]{:S(2)}) collective-permute-start(bf16[1024,128]{1,0:T(8,128)(2,1)} %get-tuple-element.128.refs_4_.refs_7_.refs_9_), channel_id=1, source_target_pairs={{0,1},{1,0},{2,3},{3,2},{4,5},{5,4},{6,7},{7,6},{8,9},{9,8},{10,11... | collective-permute-start | bytes 786440 | tf_op jit(solution)/shard_map/ppermute | solution.py:1199
  53.4 20.2 %collective-permute-start.12 = (bf16[1024,128]{1,0:T(8,128)(2,1)}, bf16[1024,128]{1,0:T(8,128)(2,1)S(1)}, u32[]{:S(2)}, u32[]{:S(2)}) collective-permute-start(bf16[1024,128]{1,0:T(8,128)(2,1)} %get-tuple-element.131.refs_5_.refs_8_.refs_10_), channel_id=1, source_target_pairs={{0,1},{1,0},{2,3},{3,2},{4,5},{5,4},{6,7},{7,6},{8,9},{9,8},{10,11... | collective-permute-start | bytes 786440 | tf_op jit(solution)/shard_map/ppermute | solution.py:1199
  92.7 14.9 %collective-permute-start.13 = (bf16[1024,128]{1,0:T(8,128)(2,1)}, bf16[1024,128]{1,0:T(8,128)(2,1)S(1)}, u32[]{:S(2)}, u32[]{:S(2)}) collective-permute-start(bf16[1024,128]{1,0:T(8,128)(2,1)} %get-tuple-element.140.refs_4_.refs_3_), channel_id=1, source_target_pairs={{0,1},{1,0},{2,3},{3,2},{4,5},{5,4},{6,7},{7,6},{8,9},{9,8},{10,11... | collective-permute-start | bytes 786440 | tf_op jit(solution)/shard_map/ppermute | solution.py:1199
  103.8 15.0 %collective-permute-start.14 = (bf16[1024,128]{1,0:T(8,128)(2,1)}, bf16[1024,128]{1,0:T(8,128)(2,1)}, u32[]{:S(2)}, u32[]{:S(2)}) collective-permute-start(bf16[1024,128]{1,0:T(8,128)(2,1)} %get-tuple-element.142.refs_5_.refs_4_), channel_id=1, source_target_pairs={{0,1},{1,0},{2,3},{3,2},{4,5},{5,4},{6,7},{7,6},{8,9},{9,8},{10,11... | collective-permute-start | bytes 786440 | tf_op jit(solution)/shard_map/ppermute | solution.py:1199
  118.8 8.1 %collective-permute-start.15 = (bf16[1024,128]{1,0:T(8,128)(2,1)}, bf16[1024,128]{1,0:T(8,128)(2,1)}, u32[]{:S(2)}, u32[]{:S(2)}) collective-permute-start(bf16[1024,128]{1,0:T(8,128)(2,1)} %get-tuple-element.144.refs_6_.refs_5_), channel_id=1, source_target_pairs={{0,1},{1,0},{2,3},{3,2},{4,5},{5,4},{6,7},{7,6},{8,9},{9,8},{10,11... | collective-permute-start | bytes 786440 | tf_op jit(solution)/shard_map/ppermute | solution.py:1199
  176.8 39.1 %collective-permute-start.17 = (bf16[192,3072]{1,0:T(8,128)(2,1)S(1)}, bf16[192,3072]{1,0:T(8,128)(2,1)S(1)}, u32[]{:S(2)}, u32[]{:S(2)}) collective-permute-start(bf16[192,3072]{1,0:T(8,128)(2,1)S(1)} %fusion.2), channel_id=1, source_target_pairs={{0,4},{2,6},{4,0},{6,2},{1,5},{3,7},{5,1},{7,3},{8,12},{10,14},{12... | collective-permute-start | bytes 3538952 | tf_op jit(solution)/shard_map/ppermute | solution.py:1199
  229.1 20.7 %collective-permute-start.18 = (bf16[1024,384]{1,0:T(8,128)(2,1)}, bf16[1024,384]{1,0:T(8,128)(2,1)S(1)}, u32[]{:S(2)}, u32[]{:S(2)}) collective-permute-start(bf16[1024,384]{1,0:T(8,128)(2,1)} %get-tuple-element.164), channel_id=1, source_target_pairs={{0,1},{1,0},{2,3},{3,2},{4,5},{5,4},{6,7},{7,6},{8,9},{9,8},{10,11... | collective-permute-start | bytes 2359304 | tf_op jit(solution)/shard_map/ppermute | solution.py:1199
  241.8 24.1 %collective-permute-start.19 = (bf16[1024,384]{1,0:T(8,128)(2,1)}, bf16[1024,384]{1,0:T(8,128)(2,1)S(1)}, u32[]{:S(2)}, u32[]{:S(2)}) collective-permute-start(bf16[1024,384]{1,0:T(8,128)(2,1)} %get-tuple-element.178.refs_2_.refs_3_), channel_id=1, source_target_pairs={{0,1},{1,0},{2,3},{3,2},{4,5},{5,4},{6,7},{7,6},{8,9},{9,8},{10,11... | collective-permute-start | bytes 2359304 | tf_op jit(solution)/shard_map/ppermute | solution.py:1199
  265.3 17.4 %collective-permute-start.20 = (bf16[2,192,1536]{2,1,0:T(8,128)(2,1)}, bf16[2,192,1536]{2,1,0:T(8,128)(2,1)}, u32[]{:S(2)}, u32[]{:S(2)}) collective-permute-start(bf16[2,192,1536]{2,1,0:T(8,128)(2,1)} %get-tuple-element.177), channel_id=1, source_target_pairs={{0,2},{2,0},{4,6},{6,4},{1,3},{3,1},{5,7},{7,5},{8,10},{10,8},{12,... | collective-permute-start | bytes 3538952 | tf_op jit(solution)/shard_map/ppermute | solution.py:1199
  265.4 58.5 %collective-permute-start.25 = (bf16[1024,384]{1,0:T(8,128)(2,1)}, bf16[1024,384]{1,0:T(8,128)(2,1)}, u32[]{:S(2)}, u32[]{:S(2)}) collective-permute-start(bf16[1024,384]{1,0:T(8,128)(2,1)} %get-tuple-element.211), channel_id=1, source_target_pairs={{0,1},{1,0},{2,3},{3,2},{4,5},{5,4},{6,7},{7,6},{8,9},{9,8},{10,11... | collective-permute-start | bytes 2359304 | tf_op jit(solution)/shard_map/ppermute | solution.py:1199
  265.9 59.7 %collective-permute-start.26 = (bf16[2048,384]{1,0:T(8,128)(2,1)}, bf16[2048,384]{1,0:T(8,128)(2,1)}, u32[]{:S(2)}, u32[]{:S(2)}) collective-permute-start(bf16[2048,384]{1,0:T(8,128)(2,1)} %get-tuple-element.215), channel_id=1, source_target_pairs={{0,1},{1,0},{2,3},{3,2},{4,5},{5,4},{6,7},{7,6},{8,9},{9,8},{10,11... | collective-permute-start | bytes 4718600 | tf_op jit(solution)/shard_map/ppermute | solution.py:1199
  284.0 17.8 %collective-permute-start.22 = (bf16[192,1536]{1,0:T(8,128)(2,1)S(1)}, bf16[192,1536]{1,0:T(8,128)(2,1)S(1)}, u32[]{:S(2)}, u32[]{:S(2)}) collective-permute-start(bf16[192,1536]{1,0:T(8,128)(2,1)S(1)} %fusion.9), channel_id=1, source_target_pairs={{0,4},{2,6},{4,0},{6,2},{1,5},{3,7},{5,1},{7,3},{8,12},{10,14},{12... | collective-permute-start | bytes 1769480 | tf_op jit(solution)/shard_map/ppermute | solution.py:1199
  301.7 13.8 %collective-permute-start.21 = (bf16[2,192,1152]{2,1,0:T(8,128)(2,1)}, bf16[2,192,1152]{2,1,0:T(8,128)(2,1)S(1)}, u32[]{:S(2)}, u32[]{:S(2)}) collective-permute-start(bf16[2,192,1152]{2,1,0:T(8,128)(2,1)} %get-tuple-element.195), channel_id=1, source_target_pairs={{0,2},{2,0},{4,6},{6,4},{1,3},{3,1},{5,7},{7,5},{8,10},{10,8},{12,... | collective-permute-start | bytes 2654216 | tf_op jit(solution)/shard_map/ppermute | solution.py:1199
  303.1 24.4 %collective-permute-start.36 = (bf16[192,1536]{1,0:T(8,128)(2,1)S(1)}, bf16[192,1536]{1,0:T(8,128)(2,1)S(1)}, u32[]{:S(2)}, u32[]{:S(2)}) collective-permute-start(bf16[192,1536]{1,0:T(8,128)(2,1)S(1)} %fusion.4), channel_id=1, source_target_pairs={{0,8},{24,16},{1,9},{25,17},{2,10},{26,18},{3,11},{27,19},{4,12},{... | collective-permute-start | bytes 1769480 | tf_op jit(solution)/shard_map/ppermute | solution.py:1232
  315.6 14.8 %collective-permute-start.23 = (bf16[192,1152]{1,0:T(8,128)(2,1)S(1)}, bf16[192,1152]{1,0:T(8,128)(2,1)S(1)}, u32[]{:S(2)}, u32[]{:S(2)}) collective-permute-start(bf16[192,1152]{1,0:T(8,128)(2,1)S(1)} %fusion.12), channel_id=1, source_target_pairs={{0,4},{2,6},{4,0},{6,2},{1,5},{3,7},{5,1},{7,3},{8,12},{10,14},{12... | collective-permute-start | bytes 1327112 | tf_op jit(solution)/shard_map/ppermute | solution.py:1199
  323.4 43.9 %collective-permute-start.24 = (bf16[1024,768]{1,0:T(8,128)(2,1)}, bf16[1024,768]{1,0:T(8,128)(2,1)S(1)}, u32[]{:S(2)}, u32[]{:S(2)}) collective-permute-start(bf16[1024,768]{1,0:T(8,128)(2,1)} %get-tuple-element.207.mine), channel_id=1, source_target_pairs={{0,1},{1,0},{2,3},{3,2},{4,5},{5,4},{6,7},{7,6},{8,9},{9,8},{10,11... | collective-permute-start | bytes 4718600 | tf_op jit(solution)/shard_map/ppermute | solution.py:1199
  327.6 22.7 %collective-permute-start.37 = (bf16[192,1536]{1,0:T(8,128)(2,1)S(1)}, bf16[192,1536]{1,0:T(8,128)(2,1)S(1)}, u32[]{:S(2)}, u32[]{:S(2)}) collective-permute-start(bf16[192,1536]{1,0:T(8,128)(2,1)S(1)} %fusion.7), channel_id=1, source_target_pairs={{8,16},{16,8},{9,17},{17,9},{10,18},{18,10},{11,19},{19,11},{12,20... | collective-permute-start | bytes 1769480 | tf_op jit(solution)/shard_map/ppermute | solution.py:1239
  328.4 11.4 %collective-permute-start.28 = (bf16[208,384]{1,0:T(8,128)(2,1)S(1)}, bf16[208,384]{1,0:T(8,128)(2,1)S(1)}, u32[]{:S(2)}, u32[]{:S(2)}) collective-permute-start(bf16[208,384]{1,0:T(8,128)(2,1)S(1)} %fusion.17), channel_id=1, source_target_pairs={{0,4},{2,6},{4,0},{6,2},{1,5},{3,7},{5,1},{7,3},{8,12},{10,14},{12... | collective-permute-start | bytes 479240 | tf_op jit(solution)/shard_map/ppermute | solution.py:1199
  330.6 21.1 %collective-permute-start.32 = (bf16[192,1152]{1,0:T(8,128)(2,1)S(1)}, bf16[192,1152]{1,0:T(8,128)(2,1)S(1)}, u32[]{:S(2)}, u32[]{:S(2)}) collective-permute-start(bf16[192,1152]{1,0:T(8,128)(2,1)S(1)} %fusion.6), channel_id=1, source_target_pairs={{0,8},{24,16},{1,9},{25,17},{2,10},{26,18},{3,11},{27,19},{4,12},{... | collective-permute-start | bytes 1327112 | tf_op jit(solution)/shard_map/ppermute | solution.py:1232
  349.0 13.8 %collective-permute-start.31 = (bf16[208,384]{1,0:T(8,128)(2,1)S(1)}, bf16[208,384]{1,0:T(8,128)(2,1)S(1)}, u32[]{:S(2)}, u32[]{:S(2)}) collective-permute-start(bf16[208,384]{1,0:T(8,128)(2,1)S(1)} %add_convert_fusion.12), channel_id=1, source_target_pairs={{8,0},{16,24},{9,1},{17,25},{10,2},{18,26},{11,3},{19,27},{12,4},{... | collective-permute-start | bytes 479240 | tf_op jit(solution)/shard_map/ppermute | solution.py:1245
  350.5 23.1 %collective-permute-start.38 = (bf16[192,1536]{1,0:T(8,128)(2,1)S(1)}, bf16[192,1536]{1,0:T(8,128)(2,1)S(1)}, u32[]{:S(2)}, u32[]{:S(2)}) collective-permute-start(bf16[192,1536]{1,0:T(8,128)(2,1)S(1)} %add_convert_fusion.4), channel_id=1, source_target_pairs={{8,0},{16,24},{9,1},{17,25},{10,2},{18,26},{11,3},{19,27},{12,4},{... | collective-permute-start | bytes 1769480 | tf_op jit(solution)/shard_map/ppermute | solution.py:1245
  351.9 10.9 %collective-permute-start.33 = (bf16[192,1152]{1,0:T(8,128)(2,1)S(1)}, bf16[192,1152]{1,0:T(8,128)(2,1)S(1)}, u32[]{:S(2)}, u32[]{:S(2)}) collective-permute-start(bf16[192,1152]{1,0:T(8,128)(2,1)S(1)} %fusion.8), channel_id=1, source_target_pairs={{8,16},{16,8},{9,17},{17,9},{10,18},{18,10},{11,19},{19,11},{12,20... | collective-permute-start | bytes 1327112 | tf_op jit(solution)/shard_map/ppermute | solution.py:1239
  364.1 16.6 %collective-permute-start.35 = (bf16[192,1152]{1,0:T(8,128)(2,1)S(1)}, bf16[192,1152]{1,0:T(8,128)(2,1)S(1)}, u32[]{:S(2)}, u32[]{:S(2)}) collective-permute-start(bf16[192,1152]{1,0:T(8,128)(2,1)S(1)} %add_convert_fusion.8), channel_id=1, source_target_pairs={{8,0},{16,24},{9,1},{17,25},{10,2},{18,26},{11,3},{19,27},{12,4},{... | collective-permute-start | bytes 1327112 | tf_op jit(solution)/shard_map/ppermute | solution.py:1245
  (61 other events, 779.7 us)
Sparse Core Ops, SparseCore 0:
  27.6 86.2 all-gather.1
  217.7 52.0 all-reduce.2
